TPU v7x, 32 devices: a whole 2x2x4 slice. The times are simulated.
32 devices in a mesh: dp: 8 (over z, y), seq: 4 (over x, core).
Axes of the slice: x: 2, y: 2, z: 4, core: 2. Of those that a mesh axis runs over, the one named last changes fastest.
Arguments:
- long_ids: int32 [24, 512], P('dp', 'seq'), may hold values from 0 to 4100
- long_targets: int32 [24, 512], P('dp', 'seq'), may hold values from 0 to 4100
- long_mask: int32 [24, 512], P('dp', 'seq'), may hold values from 0 to 1
- long_lengths: int32 [24], P('dp'), may hold values from 256 to 512, as said below
- short_ids: int32 [64, 128], P(('dp', 'seq')), may hold values from 0 to 4100
- short_targets: int32 [64, 128], P(('dp', 'seq')), may hold values from 0 to 4100
- short_mask: int32 [64, 128], P(('dp', 'seq')), may hold values from 0 to 1
- short_lengths: int32 [64], P(('dp', 'seq')), may hold values from 64 to 128, as said below
- table: float32 [4101, 768], P(None, ('dp', 'seq')), may hold values from -0.21875 to 0.21875
- position: float32 [512, 768], P(None, ('dp', 'seq')), may hold values from -0.21875 to 0.21875
- qkv_weight: float32 [768, 2304], P(('dp', 'seq')), may hold values from -0.21875 to 0.21875
- out_weight: float32 [768, 768], P(('dp', 'seq')), may hold values from -1.75 to 1.75
- in_weight: float32 [768, 3072], P(('dp', 'seq')), may hold values from -0.21875 to 0.21875
- down_weight: float32 [3072, 768], P(('dp', 'seq')), may hold values from -0.109375 to 0.109375
- norms: float32 [768, 6], P(('dp', 'seq')), may hold values from -1 to 3, as said below
- table_rows: float32 [4101], replicated, may hold values from 1.5875193e-08 to 6.350077e-08
- table_cols: float32 [768], P(('dp', 'seq')), may hold values from 1.5875193e-08 to 6.350077e-08
- position_rows: float32 [512], replicated, may hold values from 2.4283373e-09 to 9.713349e-09
- position_cols: float32 [768], P(('dp', 'seq')), may hold values from 2.4283373e-09 to 9.713349e-09
- qkv_rows: float32 [768], P(('dp', 'seq')), may hold values from 8.477105e-08 to 3.390842e-07
- qkv_cols: float32 [2304], replicated, may hold values from 8.477105e-08 to 3.390842e-07
- out_rows: float32 [768], P(('dp', 'seq')), may hold values from 8.477105e-08 to 3.390842e-07
- out_cols: float32 [768], replicated, may hold values from 8.477105e-08 to 3.390842e-07
- in_rows: float32 [768], P(('dp', 'seq')), may hold values from 8.477105e-08 to 3.390842e-07
- in_cols: float32 [3072], replicated, may hold values from 8.477105e-08 to 3.390842e-07
- down_rows: float32 [3072], P(('dp', 'seq')), may hold values from 8.477105e-08 to 3.390842e-07
- down_cols: float32 [768], replicated, may hold values from 8.477105e-08 to 3.390842e-07
- norm_moment: float32 [768, 6], P(('dp', 'seq')), may hold values from 8.477105e-08 to 3.390842e-07
Outputs:
- loss_sum: float32 [], replicated
- mask_count: float32 [], replicated
- table_grad: float32 [4101, 768], P(None, ('dp', 'seq'))
- position_grad: float32 [512, 768], P(None, ('dp', 'seq'))
- qkv_grad: float32 [768, 2304], P(('dp', 'seq'))
- out_grad: float32 [768, 768], P(('dp', 'seq'))
- in_grad: float32 [768, 3072], P(('dp', 'seq'))
- down_grad: float32 [3072, 768], P(('dp', 'seq'))
- norm_grad: float32 [768, 6], P(('dp', 'seq'))
- table_rows_new: float32 [4101], replicated
- table_cols_new: float32 [768], P(('dp', 'seq'))
- position_rows_new: float32 [512], replicated
- position_cols_new: float32 [768], P(('dp', 'seq'))
- qkv_rows_new: float32 [768], P(('dp', 'seq'))
- qkv_cols_new: float32 [2304], replicated
- out_rows_new: float32 [768], P(('dp', 'seq'))
- out_cols_new: float32 [768], replicated
- in_rows_new: float32 [768], P(('dp', 'seq'))
- in_cols_new: float32 [3072], replicated
- down_rows_new: float32 [3072], P(('dp', 'seq'))
- down_cols_new: float32 [768], replicated
- norm_moment_new: float32 [768, 6], P(('dp', 'seq'))
- table_new: float32 [4101, 768], P(None, ('dp', 'seq'))
- position_new: float32 [512, 768], P(None, ('dp', 'seq'))
- qkv_new: float32 [768, 2304], P(('dp', 'seq'))
- out_new: float32 [768, 768], P(('dp', 'seq'))
- in_new: float32 [768, 3072], P(('dp', 'seq'))
- down_new: float32 [3072, 768], P(('dp', 'seq'))
- norm_new: float32 [768, 6], P(('dp', 'seq'))
Inputs may be any that keep to these rules, and one draw needn't show every extreme that they name: `long_lengths`: in every aligned block of 3 rows one row has length 512. `short_lengths`: in every aligned block of 2 rows one row has length 128. `norms`: columns 0, 2 and 4 are positive gains, columns 1, 3 and 5 shifts.
All inputs are finite; a program needn't handle non-finite values.
Results may differ from a plain program's by a relative error of at most 0.0085.
The roundings to bfloat16 on the way count: a program that leaves them out, or rounds other values in their place, can miss the bound.
Values may be sent and summed in bfloat16 or wider, within the bound.
A program may use at most 192 MiB of HBM per device.

v0:
```python
import jax
import jax.numpy as jnp
from jax import lax
from jax.sharding import PartitionSpec as P

D = 768
HEADS = 12
HEAD_DIM = 64
STEP = 10


EPSILON = 1e-12
SQUARE_FLOOR = 1e-30
learn_rate = 0.3


def gelu_pair(hidden):
    normal_cdf = 0.5 * (1.0 + lax.erf(hidden * 0.7071067811865476))
    return (
        hidden * normal_cdf,
        normal_cdf + hidden * jnp.exp(-0.5 * hidden * hidden) * 0.3989422804014327,
    )


def norm_forward(value, gain, shift):
    centred = value - jnp.mean(value, -1, keepdims=True)
    inverse = lax.rsqrt(jnp.mean(centred * centred, -1, keepdims=True) + EPSILON)
    normed = centred * inverse
    return (normed * gain + shift, normed, inverse)


def norm_backward(grad_out, normed, inverse, gain):
    scaled = grad_out * gain
    back = inverse * (
        scaled
        - jnp.mean(scaled, -1, keepdims=True)
        - normed * jnp.mean(scaled * normed, -1, keepdims=True)
    )
    return (back, jnp.sum(grad_out * normed, (0, 1)), jnp.sum(grad_out, (0, 1)))


def score_of(query_h, key_h, keep_row):
    scores = (
        jnp.einsum("bqhe,bkhe->bhqk", query_h, key_h, preferred_element_type=jnp.float32) * 0.125
    )
    return jnp.where(keep_row[:, None, None, :], scores, -1e30)


def attend(query_h, key_h, value_h, keep_row):
    scores = score_of(query_h, key_h, keep_row)
    highest = jnp.max(scores, -1, keepdims=True)
    raised = jnp.exp(scores - highest)
    summed = jnp.sum(raised, -1, keepdims=True)
    shares = (raised / summed).astype(jnp.bfloat16)
    mixture = jnp.einsum("bhqk,bkhe->bqhe", shares, value_h, preferred_element_type=jnp.float32)
    return (mixture.astype(jnp.bfloat16), highest + jnp.log(summed))


def attend_back(query_h, key_h, value_h, keep_row, log_total, grad_mix):
    shares = jnp.exp(score_of(query_h, key_h, keep_row) - log_total)
    grad_share = jnp.einsum(
        "bqhe,bkhe->bhqk", grad_mix, value_h, preferred_element_type=jnp.float32
    )
    grad_score = (shares * (grad_share - jnp.sum(shares * grad_share, -1, keepdims=True))).astype(
        jnp.bfloat16
    )
    grad_query = (
        jnp.einsum("bhqk,bkhe->bqhe", grad_score, key_h, preferred_element_type=jnp.float32) * 0.125
    )
    grad_key = (
        jnp.einsum("bhqk,bqhe->bkhe", grad_score, query_h, preferred_element_type=jnp.float32)
        * 0.125
    )
    grad_value = jnp.einsum(
        "bhqk,bqhe->bkhe", shares.astype(jnp.bfloat16), grad_mix, preferred_element_type=jnp.float32
    )
    return jnp.stack((grad_query, grad_key, grad_value), 2).astype(jnp.bfloat16)


def heads_forward(qkv_b, keep_row, spread):
    row_count, tok_count = (qkv_b.shape[0], qkv_b.shape[1])
    if spread:
        groups = lax.axis_size("seq")
        pieces = lax.all_to_all(
            qkv_b.reshape(row_count, tok_count, 3, groups, D // groups),
            "seq",
            split_axis=3,
            concat_axis=1,
            tiled=True,
        )
        by_head = pieces.reshape(row_count, tok_count * groups, 3, HEADS // groups, HEAD_DIM)
    else:
        by_head = qkv_b.reshape(row_count, tok_count, 3, HEADS, HEAD_DIM)
    mixture, log_total = attend(by_head[:, :, 0], by_head[:, :, 1], by_head[:, :, 2], keep_row)
    if spread:
        mixture = lax.all_to_all(
            mixture.reshape(row_count, tok_count * groups, 1, D // groups),
            "seq",
            split_axis=1,
            concat_axis=2,
            tiled=True,
        )
    return (mixture.reshape(row_count, tok_count, D), by_head, log_total)


def heads_backward(by_head, keep_row, log_total, grad_mix, spread):
    row_count, tok_count = (grad_mix.shape[0], grad_mix.shape[1])
    full_len = by_head.shape[1]
    if spread:
        groups = lax.axis_size("seq")
        grad_mix = lax.all_to_all(
            grad_mix.reshape(row_count, tok_count, groups, D // groups),
            "seq",
            split_axis=2,
            concat_axis=1,
            tiled=True,
        )
    grad_mix = grad_mix.reshape(row_count, full_len, by_head.shape[3], HEAD_DIM)
    stacked = attend_back(
        by_head[:, :, 0], by_head[:, :, 1], by_head[:, :, 2], keep_row, log_total, grad_mix
    )
    if spread:
        stacked = lax.all_to_all(
            stacked.reshape(row_count, full_len, 3, 1, D // groups),
            "seq",
            split_axis=1,
            concat_axis=3,
            tiled=True,
        )
    return stacked.reshape(row_count, tok_count, 3 * D)


def bucket_step(
    weights, tables, ids, targets, weight, keep_row, offset, spread, inverse_count, ffn_hook=None
):
    qkv_w, out_w, in_w, down_w, norms_b = weights
    table, place = tables
    gains = norms_b.astype(jnp.float32)
    tok_count = ids.shape[1]
    place_rows = lax.dynamic_slice_in_dim(place, offset, tok_count, 0)
    embedded = table[ids].astype(jnp.float32) + place_rows.astype(jnp.float32)[None]
    first, normed_a, inverse_a = norm_forward(embedded, gains[:, 0], gains[:, 1])
    first_b = first.astype(jnp.bfloat16)
    qkv_b = jnp.einsum("btd,de->bte", first_b, qkv_w, preferred_element_type=jnp.float32).astype(
        jnp.bfloat16
    )
    mixture, by_head, log_total = heads_forward(qkv_b, keep_row, spread)
    attn_out = jnp.einsum("btd,de->bte", mixture, out_w, preferred_element_type=jnp.float32)
    second, normed_b, inverse_b = norm_forward(first + attn_out, gains[:, 2], gains[:, 3])
    second_b = second.astype(jnp.bfloat16)
    hidden = jnp.einsum("btd,df->btf", second_b, in_w, preferred_element_type=jnp.float32)
    active, slope = gelu_pair(hidden)
    active_b = active.astype(jnp.bfloat16)
    ffn_out = jnp.einsum("btf,fd->btd", active_b, down_w, preferred_element_type=jnp.float32)
    third, normed_c, inverse_c = norm_forward(second + ffn_out, gains[:, 4], gains[:, 5])
    third_b = third.astype(jnp.bfloat16)
    logits = jnp.einsum("btd,vd->btv", third_b, table, preferred_element_type=jnp.float32)
    highest = jnp.max(logits, -1, keepdims=True)
    log_sum = highest + jnp.log(jnp.sum(jnp.exp(logits - highest), -1, keepdims=True))
    picked = jnp.take_along_axis(logits, targets[..., None], -1)
    loss_part = jnp.sum(weight * (log_sum - picked)[..., 0])
    onehot = (
        targets[..., None] == lax.broadcasted_iota(jnp.int32, (1, 1, logits.shape[2]), 2)
    ).astype(jnp.float32)
    grad_logit = (
        (jnp.exp(logits - log_sum) - onehot) * (weight * inverse_count)[..., None]
    ).astype(jnp.bfloat16)
    grad_third = jnp.einsum("btv,vd->btd", grad_logit, table, preferred_element_type=jnp.float32)
    table_grad = jnp.einsum("btv,btd->vd", grad_logit, third_b, preferred_element_type=jnp.float32)
    grad_second, gain_c, shift_c = norm_backward(grad_third, normed_c, inverse_c, gains[:, 4])
    grad_ffn = grad_second.astype(jnp.bfloat16)
    down_grad = jnp.einsum("btf,btd->fd", active_b, grad_ffn, preferred_element_type=jnp.float32)
    grad_hidden = (
        jnp.einsum("btd,fd->btf", grad_ffn, down_w, preferred_element_type=jnp.float32) * slope
    ).astype(jnp.bfloat16)
    in_grad = jnp.einsum("btd,btf->df", second_b, grad_hidden, preferred_element_type=jnp.float32)
    grad_second = grad_second + jnp.einsum(
        "btf,df->btd", grad_hidden, in_w, preferred_element_type=jnp.float32
    )
    grad_first, gain_b, shift_b = norm_backward(grad_second, normed_b, inverse_b, gains[:, 2])
    grad_attn = grad_first.astype(jnp.bfloat16)
    out_grad = jnp.einsum("btd,bte->de", mixture, grad_attn, preferred_element_type=jnp.float32)
    grad_mix = jnp.einsum(
        "bte,de->btd", grad_attn, out_w, preferred_element_type=jnp.float32
    ).astype(jnp.bfloat16)
    grad_qkv = heads_backward(by_head, keep_row, log_total, grad_mix, spread)
    qkv_grad = jnp.einsum("btd,bte->de", first_b, grad_qkv, preferred_element_type=jnp.float32)
    grad_first = grad_first + jnp.einsum(
        "bte,de->btd", grad_qkv, qkv_w, preferred_element_type=jnp.float32
    )
    grad_embed, gain_a, shift_a = norm_backward(grad_first, normed_a, inverse_a, gains[:, 0])
    flat_rows = grad_embed.reshape(-1, grad_embed.shape[2])
    table_grad = table_grad.at[ids.reshape(-1)].add(flat_rows)
    place_grad = lax.dynamic_update_slice_in_dim(
        jnp.zeros(place.shape, jnp.float32), jnp.sum(grad_embed, 0), offset, 0
    )
    norm_grad = jnp.stack((gain_a, shift_a, gain_b, shift_b, gain_c, shift_c), 1)
    return (loss_part, (table_grad, place_grad, qkv_grad, out_grad, in_grad, down_grad, norm_grad))


def reduce_once(grads):
    row_parts = (
        lax.psum_scatter(grads[2], ("dp", "seq"), scatter_dimension=0, tiled=True),
        lax.psum_scatter(grads[3], ("dp", "seq"), scatter_dimension=0, tiled=True),
        lax.psum_scatter(grads[4], ("dp", "seq"), scatter_dimension=0, tiled=True),
        lax.psum_scatter(grads[5], ("dp", "seq"), scatter_dimension=0, tiled=True),
        lax.psum_scatter(grads[6], ("dp", "seq"), scatter_dimension=0, tiled=True),
    )
    table_parts = (
        lax.psum_scatter(grads[0], ("dp", "seq"), scatter_dimension=1, tiled=True),
        lax.psum_scatter(grads[1], ("dp", "seq"), scatter_dimension=1, tiled=True),
    )
    return (
        table_parts[0],
        table_parts[1],
        row_parts[0],
        row_parts[1],
        row_parts[2],
        row_parts[3],
        row_parts[4],
    )


def on_device(
    long_ids,
    long_targets,
    long_mask,
    long_lengths,
    short_ids,
    short_targets,
    short_mask,
    short_lengths,
    table,
    position,
    qkv_weight,
    out_weight,
    in_weight,
    down_weight,
    norms,
    table_rows,
    table_cols,
    position_rows,
    position_cols,
    qkv_rows,
    qkv_cols,
    out_rows,
    out_cols,
    in_rows,
    in_cols,
    down_rows,
    down_cols,
    norm_moment,
):
    devices = lax.axis_size(("dp", "seq"))
    seq_index = lax.axis_index("seq")
    weights = (
        lax.all_gather(qkv_weight.astype(jnp.bfloat16), ("dp", "seq"), axis=0, tiled=True),
        lax.all_gather(out_weight.astype(jnp.bfloat16), ("dp", "seq"), axis=0, tiled=True),
        lax.all_gather(in_weight.astype(jnp.bfloat16), ("dp", "seq"), axis=0, tiled=True),
        lax.all_gather(down_weight.astype(jnp.bfloat16), ("dp", "seq"), axis=0, tiled=True),
        lax.all_gather(norms.astype(jnp.bfloat16), ("dp", "seq"), axis=0, tiled=True),
    )
    tables = (
        lax.all_gather(table.astype(jnp.bfloat16), ("dp", "seq"), axis=1, tiled=True),
        lax.all_gather(position.astype(jnp.bfloat16), ("dp", "seq"), axis=1, tiled=True),
    )
    long_count = long_ids.shape[1]
    long_offset = seq_index * long_count
    long_place = long_offset + lax.iota(jnp.int32, long_count)
    long_weight = long_mask.astype(jnp.float32) * (
        long_place[None, :] < long_lengths[:, None]
    ).astype(jnp.float32)
    long_keep = (
        lax.iota(jnp.int32, long_count * lax.axis_size("seq"))[None, :] < long_lengths[:, None]
    )
    short_keep = lax.iota(jnp.int32, short_ids.shape[1])[None, :] < short_lengths[:, None]
    short_weight = short_mask.astype(jnp.float32) * short_keep.astype(jnp.float32)
    mask_count = lax.psum(jnp.sum(long_weight) + jnp.sum(short_weight), ("dp", "seq"))
    inverse_count = 1.0 / mask_count
    long_loss, long_grads = bucket_step(
        weights,
        tables,
        long_ids,
        long_targets,
        long_weight,
        long_keep,
        long_offset,
        True,
        inverse_count,
    )
    short_loss, short_grads = bucket_step(
        weights, tables, short_ids, short_targets, short_weight, short_keep, 0, False, inverse_count
    )
    summed = reduce_once(
        tuple(
            (first_part + second_part for first_part, second_part in zip(long_grads, short_grads))
        )
    )
    decay = 1.0 - STEP ** (-0.8)
    table_g, place_g, qkv_g, out_g, in_g, down_g, norm_g = summed
    matrices = (
        (qkv_weight, qkv_g, qkv_rows, qkv_cols),
        (out_weight, out_g, out_rows, out_cols),
        (in_weight, in_g, in_rows, in_cols),
        (down_weight, down_g, down_rows, down_cols),
    )
    wide = (
        (table, table_g, table_rows, table_cols),
        (position, place_g, position_rows, position_cols),
    )
    row_news = [
        decay * member[2] + (1.0 - decay) * jnp.mean(member[1] * member[1] + SQUARE_FLOOR, 1)
        for member in matrices
    ]
    col_parts = [jnp.sum(member[1] * member[1] + SQUARE_FLOOR, 0) for member in matrices]
    row_totals = jnp.stack([jnp.sum(rows_new) for rows_new in row_news])
    wide_parts = [jnp.sum(member[1] * member[1] + SQUARE_FLOOR, 1) for member in wide]
    wide_cols = [
        decay * member[3] + (1.0 - decay) * jnp.mean(member[1] * member[1] + SQUARE_FLOOR, 0)
        for member in wide
    ]
    weight_sq = jnp.stack([jnp.sum(member[0] * member[0]) for member in matrices + wide])
    norm_sq = jnp.sum(norms * norms, 0)
    stats = lax.psum(
        (
            col_parts[0],
            col_parts[1],
            col_parts[2],
            col_parts[3],
            wide_parts[0],
            wide_parts[1],
            row_totals,
            weight_sq,
            norm_sq,
            long_loss + short_loss,
        ),
        ("dp", "seq"),
    )
    updates = []
    rows_out = []
    cols_out = []
    for index in range(4):
        member = matrices[index]
        full_rows = member[0].shape[0] * devices
        cols_new = decay * member[3] + (1.0 - decay) * stats[index] / full_rows
        rows_mean = stats[6][index] / full_rows
        update = member[1] * lax.rsqrt(row_news[index][:, None] * cols_new[None, :] / rows_mean)
        updates.append(update)
        rows_out.append(row_news[index])
        cols_out.append(cols_new)
    for index in range(2):
        member = wide[index]
        rows_new = decay * member[2] + (1.0 - decay) * stats[4 + index] / D
        update = member[1] * lax.rsqrt(
            rows_new[:, None] * wide_cols[index][None, :] / jnp.mean(rows_new)
        )
        updates.append(update)
        rows_out.append(rows_new)
        cols_out.append(wide_cols[index])
    moment_new = decay * norm_moment + (1.0 - decay) * (norm_g * norm_g + SQUARE_FLOOR)
    norm_update = norm_g * lax.rsqrt(moment_new)
    update_sq = jnp.stack([jnp.sum(update * update) for update in updates])
    totals = lax.psum((update_sq, jnp.sum(norm_update * norm_update, 0)), ("dp", "seq"))
    owners = [member[0] for member in matrices + wide]
    new_weights = []
    for index in range(6):
        entries = owners[index].shape[0] * owners[index].shape[1] * devices
        clip = jnp.maximum(1.0, jnp.sqrt(totals[0][index] / entries))
        new_weights.append(
            owners[index] - learn_rate * jnp.sqrt(stats[7][index] / entries) * updates[index] / clip
        )
    norm_rows = norms.shape[0] * devices
    norm_clip = jnp.maximum(1.0, jnp.sqrt(totals[1] / norm_rows))
    norm_new = norms - learn_rate * jnp.sqrt(stats[8] / norm_rows) * norm_update / norm_clip
    return (
        stats[9],
        mask_count,
        table_g,
        place_g,
        qkv_g,
        out_g,
        in_g,
        down_g,
        norm_g,
        rows_out[4],
        cols_out[4],
        rows_out[5],
        cols_out[5],
        rows_out[0],
        cols_out[0],
        rows_out[1],
        cols_out[1],
        rows_out[2],
        cols_out[2],
        rows_out[3],
        cols_out[3],
        moment_new,
        new_weights[4],
        new_weights[5],
        new_weights[0],
        new_weights[1],
        new_weights[2],
        new_weights[3],
        norm_new,
    )


def solution(mesh):
    return jax.shard_map(
        on_device,
        mesh=mesh,
        in_specs=(
            P("dp", "seq"),
            P("dp", "seq"),
            P("dp", "seq"),
            P("dp"),
            P(("dp", "seq"), None),
            P(("dp", "seq"), None),
            P(("dp", "seq"), None),
            P(("dp", "seq")),
            P(None, ("dp", "seq")),
            P(None, ("dp", "seq")),
            P(("dp", "seq"), None),
            P(("dp", "seq"), None),
            P(("dp", "seq"), None),
            P(("dp", "seq"), None),
            P(("dp", "seq"), None),
            P(),
            P(("dp", "seq")),
            P(),
            P(("dp", "seq")),
            P(("dp", "seq")),
            P(),
            P(("dp", "seq")),
            P(),
            P(("dp", "seq")),
            P(),
            P(("dp", "seq")),
            P(),
            P(("dp", "seq"), None),
        ),
        out_specs=(
            P(),
            P(),
            P(None, ("dp", "seq")),
            P(None, ("dp", "seq")),
            P(("dp", "seq"), None),
            P(("dp", "seq"), None),
            P(("dp", "seq"), None),
            P(("dp", "seq"), None),
            P(("dp", "seq"), None),
            P(),
            P(("dp", "seq")),
            P(),
            P(("dp", "seq")),
            P(("dp", "seq")),
            P(),
            P(("dp", "seq")),
            P(),
            P(("dp", "seq")),
            P(),
            P(("dp", "seq")),
            P(),
            P(("dp", "seq"), None),
            P(None, ("dp", "seq")),
            P(None, ("dp", "seq")),
            P(("dp", "seq"), None),
            P(("dp", "seq"), None),
            P(("dp", "seq"), None),
            P(("dp", "seq"), None),
            P(("dp", "seq"), None),
        ),
        check_vma=False,
    )
```

profile of v0, /device:TPU:0, one launch (start us, length us, event | category | flops | bytes accessed | tf_op | source)
XLA Modules:
  0.0 1536.5 jit_solution(11013092494278976979)
XLA Ops:
  18.9 43.7 %all-gather = bf16[32,24,6]{1,2,0:T(8,128)(2,1)S(1)} all-gather(bf16[1,24,6]{1,2,0:T(8,128)(2,1)S(1)} %get-tuple-element.297), channel_id=1, replica_groups=mesh['dp'=8,'seq'=4] {'dp','seq'}, dimensions={0}, use_global_device_ids=true | all-gather | bytes 9504 | tf_op jit(solution)/shard_map/all_gather | solution.py:261
  63.6 40.2 %all_gather.22 = bf16[512,768]{0,1:T(8,128)(2,1)S(1)} all-gather(bf16[512,24]{0,1:T(8,128)(2,1)S(1)} %get-tuple-element.295), channel_id=1, replica_groups=mesh['dp'=8,'seq'=4] {'dp','seq'}, dimensions={1}, use_global_device_ids=true | all-gather | bytes 811008 | tf_op jit(solution)/shard_map/all_gather | solution.py:265
  104.6 9.3 copy.269
  113.9 6.2 gather_fusion
  120.7 30.1 %all-gather.9.cloned.1.call-done = bf16[768,2304]{1,0:T(8,128)(2,1)} async-done(((bf16[24,2304]{1,0:T(8,128)(2,1)}), bf16[768,2304]{1,0:T(8,128)(2,1)}) %all-gather.9.cloned.1.call-update) | async-done | bytes 3538960 | tf_op jit(solution)/shard_map/all_gather | solution.py:257
  150.8 5.0 convolution_convert_fusion
  159.9 4.6 all-to-all-start
  164.5 5.0 gather_fusion.1
  169.9 3.2 convolution_convert_fusion.1
  178.7 29.2 %all-gather.11.cloned.1.call-done = bf16[768,768]{1,0:T(8,128)(2,1)} async-done(((bf16[24,768]{1,0:T(8,128)(2,1)}), bf16[768,768]{1,0:T(8,128)(2,1)}) %all-gather.11.cloned.1.call-update) | async-done | bytes 1179664 | tf_op jit(solution)/shard_map/all_gather | solution.py:258
  210.3 63.6 %all-gather.13.cloned.1.call-done = bf16[768,3072]{1,0:T(8,128)(2,1)} async-done(((bf16[24,3072]{1,0:T(8,128)(2,1)}), bf16[768,3072]{1,0:T(8,128)(2,1)}) %all-gather.13.cloned.1.call-update) | async-done | bytes 4718608 | tf_op jit(solution)/shard_map/all_gather | solution.py:259
  273.9 5.5 fusion.30
  279.3 60.3 %all-gather.15.cloned.1.call-done = bf16[3072,768]{1,0:T(8,128)(2,1)} async-done(((bf16[96,768]{1,0:T(8,128)(2,1)}), bf16[3072,768]{1,0:T(8,128)(2,1)}) %all-gather.15.cloned.1.call-update) | async-done | bytes 4718608 | tf_op jit(solution)/shard_map/all_gather | solution.py:260
  339.7 4.8 fusion.211
  344.7 9.5 fusion.212
  354.3 3.9 gather_fusion.3
  360.9 4.1 copy.275
  365.0 4.0 reshape.553
  369.0 3.3 fusion.42
  375.9 4.4 fusion.71
  382.6 4.7 all-to-all-start.1
  388.1 13.7 all-to-all-done.1
  408.3 6.5 multiply_convert_fusion.2
  417.3 9.4 fusion.208
  426.7 5.3 gather_fusion.2
  432.1 3.6 exponential_reduce_fusion
  437.7 39.8 %psum.92 = f32[]{:T(128)} all-reduce(f32[]{:T(128)S(6)} %add.454), channel_id=1, replica_groups=mesh['dp'=8,'seq'=4] {'dp','seq'}, use_global_device_ids=true, to_apply=%region_25.26 | all-reduce | flops 1 | bytes 8 | tf_op jit(solution)/shard_map/psum | solution.py:278
  478.4 7.9 multiply_reduce_fusion.12
  488.6 5.2 multiply_reduce_fusion.13
  498.4 9.9 multiply_reduce_fusion.3
  508.7 3.4 fusion.15
  524.0 4.2 all-to-all-start.2
  528.2 3.9 bitcast_add_fusion.4
  544.0 7.0 fusion.72
  551.1 6.3 multiply_reduce_fusion
  564.1 3.7 copy.297
  567.8 4.8 copy.296
  572.6 4.8 copy.295
  577.4 8.3 pad_maximum_fusion
  585.7 4.8 all-to-all-start.3
  597.1 31.9 %all-to-all-done.3 = bf16[3,512,3,1,192]{4,2,0,3,1:T(4,128)(2,1)} async-done(((bf16[3,512,3,1,192]{4,2,0,3,1:T(4,128)(2,1)}), bf16[3,512,3,1,192]{4,2,0,3,1:T(4,128)(2,1)}, u32[]{:S(2)}, u32[]{:S(2)}) %all-to-all-start.3) | async-done | bytes 1769504 | tf_op jit(solution)/shard_map/all_to_all | solution.py:123
  629.1 6.0 copy.342
  637.1 5.3 fusion.104
  648.0 7.2 fusion.160
  655.2 6.4 bitcast_add_fusion
  661.6 17.5 %scatter_custom_fusion = f32[4101,768]{1,0:T(8,128)} fusion(f32[4101,768]{1,0:T(8,128)} %bitcast_add_fusion, s32[640]{0:T(1024)S(1)} %add_reduce_fusion, f32[256,768]{1,0:T(8,128)} %bitcast.327, f32[]{:T(128)} %constant.217.clone.1, f32[384,768]{1,0:T(8,128)} %bitcast.333), kind=kCustom, calls=%fused_computation.83 | custom fusion | flops 983040 | bytes 14564864 | tf_op jit(solution)/shard_map/add | solution.py:296
  682.2 5.3 bitcast_add_fusion.3
  688.8 4.5 fusion.138
  693.3 4.6 bitcast_add_fusion.1
  699.2 4.5 fusion.157
  703.7 5.2 bitcast_add_fusion.2
  712.0 4.5 stack.155
  720.8 23.5 %reduce-scatter.18.cloned.1.call-done = f32[24,512]{1,0:T(8,128)} async-done(((f32[768,512]{1,0:T(8,128)}), f32[24,512]{1,0:T(8,128)}) %reduce-scatter.18.cloned.1.call-update) | async-done | bytes 49168
  746.5 236.3 %all-reduce.7.cloned.1.call-done = f32[4101,768]{1,0:T(8,128)} async-done(((f32[4101,768]{1,0:T(8,128)}), f32[4101,768]{1,0:T(8,128)}) %all-reduce.7.cloned.1.call-update) | async-done | bytes 12598288
  982.8 3.4 fusion.59
  988.1 119.4 %reduce-scatter.10.cloned.1.call-done = f32[24,2304]{1,0:T(8,128)} async-done(((f32[768,2304]{1,0:T(8,128)}), f32[24,2304]{1,0:T(8,128)}) %reduce-scatter.10.cloned.1.call-update) | async-done | bytes 221200 | tf_op jit(solution)/shard_map/reduce_scatter | solution.py:203
  1110.2 139.5 %reduce-scatter.16.cloned.1.call-done = f32[96,768]{1,0:T(8,128)} async-done(((f32[3072,768]{1,0:T(8,128)}), f32[96,768]{1,0:T(8,128)}) %reduce-scatter.16.cloned.1.call-update) | async-done | bytes 294928 | tf_op jit(solution)/shard_map/reduce_scatter | solution.py:206
  1252.6 138.3 %reduce-scatter.14.cloned.1.call-done = f32[24,3072]{1,0:T(8,128)} async-done(((f32[768,3072]{1,0:T(8,128)}), f32[24,3072]{1,0:T(8,128)}) %reduce-scatter.14.cloned.1.call-update) | async-done | bytes 294928 | tf_op jit(solution)/shard_map/reduce_scatter | solution.py:205
  1394.3 3.2 pad_maximum_fusion.2
  1397.4 42.5 %all-reduce.4 = (f32[768,6]{0,1:T(8,128)}, f32[4101]{0:T(1024)}, f32[512]{0:T(512)}, f32[2304]{0:T(1024)}, f32[768]{0:T(1024)}, /*index=5*/f32[3072]{0:T(1024)}, f32[768]{0:T(1024)}, f32[4]{0:T(128)}) all-reduce(f32[768,6]{0,1:T(8,128)S(1)} %add.474, ...), channel_id=8, replica_groups=mesh['dp'=8,'seq'=4] {'dp','seq'}, use_global_device_ids=true, to_apply=%region_61.62.clone | all-reduce | flops 16137 | bytes 129096
  1461.5 4.5 stack.167
  1466.0 39.8 %all-reduce.3 = (f32[]{:T(128)}, f32[6]{0:T(128)}, f32[6]{0:T(128)}, f32[6]{0:T(128)}, f32[6]{0:T(128)}) all-reduce(f32[]{:T(128)S(6)} %add.453, f32[6]{0:T(128)} %stack.167, f32[6]{0:T(128)} %stack.155, f32[6]{0:T(128)} %get-tuple-element.262, f32[6]{0:T(128)} %get-tuple-element.296), channel_id=1, replica_groups=mesh['dp'=8,'seq'=4] {'dp','seq'}, use_global_device_ids=true, to_apply=%region_22.23 | all-reduce | flops 25 | bytes 200 | tf_op jit(solution)/shard_map/psum | solution.py:324
  1510.3 4.1 divide_subtract_fusion
  1514.5 3.1 copy.319
  (460 shorter events, 146.9 us)
Async XLA Ops:
  7.2 11.0 copy-start.70
  7.2 55.7 %copy-start.48 = (f32[512,24]{0,1:T(8,128)S(1)}, f32[512,24]{0,1:T(8,128)}, u32[]{:S(2)}) copy-start(f32[512,24]{0,1:T(8,128)} %param.37) | copy-start | bytes 147460
  7.2 97.4 %all-gather.7.cloned.1.call-start = ((), (), s32[]{:S(2)}) async-start(), calls=%async_computation.9 | async-start | bytes 6690816 | tf_op jit(solution)/shard_map/all_gather | solution.py:264
  9.8 141.0 %all-gather.9.cloned.1.call-start = ((), (), s32[]{:S(2)}) async-start(), calls=%async_computation.10 | async-start | bytes 3649536 | tf_op jit(solution)/shard_map/all_gather | solution.py:257
  12.2 195.8 %all-gather.11.cloned.1.call-start = ((), (), s32[]{:S(2)}) async-start(), calls=%async_computation.11 | async-start | bytes 1216512 | tf_op jit(solution)/shard_map/all_gather | solution.py:258
  14.4 259.4 %all-gather.13.cloned.1.call-start = ((), (), s32[]{:S(2)}) async-start(), calls=%async_computation.12 | async-start | bytes 4866048 | tf_op jit(solution)/shard_map/all_gather | solution.py:259
  16.8 322.8 %all-gather.15.cloned.1.call-start = ((), (), s32[]{:S(2)}) async-start(), calls=%async_computation.13 | async-start | bytes 4866048 | tf_op jit(solution)/shard_map/all_gather | solution.py:260
  18.2 86.0 %copy-start.67 = (s32[2,128]{1,0:T(2,128)S(1)}, s32[2,128]{1,0:T(2,128)}, u32[]{:S(2)}) copy-start(s32[2,128]{1,0:T(2,128)} %param.33) | copy-start | bytes 3076
  18.2 86.1 %copy-start.72 = (s32[3,128]{1,0:T(4,128)S(1)}, s32[3,128]{1,0:T(4,128)}, u32[]{:S(2)}) copy-start(s32[3,128]{1,0:T(4,128)} %param.28) | copy-start | bytes 4612
  18.2 86.1 %copy-start.97 = (s32[2,128]{1,0:T(2,128)S(1)}, s32[2,128]{1,0:T(2,128)}, u32[]{:S(2)}) copy-start(s32[2,128]{1,0:T(2,128)} %param.32) | copy-start | bytes 3076
  18.2 86.1 %copy-start.64 = (s32[3,128]{1,0:T(4,128)S(1)}, s32[3,128]{1,0:T(4,128)}, u32[]{:S(2)}) copy-start(s32[3,128]{1,0:T(4,128)} %param.29) | copy-start | bytes 4612
  18.2 86.2 %copy-start.101 = (s32[2]{0:T(128)S(1)}, s32[2]{0:T(128)}, u32[]{:S(2)}) copy-start(s32[2]{0:T(128)} %param.35) | copy-start | bytes 28
  18.2 86.3 %copy-start.81 = (s32[3]{0:T(128)S(1)}, s32[3]{0:T(128)}, u32[]{:S(2)}) copy-start(s32[3]{0:T(128)} %param.31) | copy-start | bytes 40
  104.0 46.8 %copy-start.9 = (f32[128,768]{1,0:T(8,128)}, f32[128,768]{1,0:T(8,128)S(1)}, u32[]{:S(2)}) copy-start(f32[128,768]{1,0:T(8,128)S(1)} %copy.270) | copy-start | bytes 1179652
  159.9 201.0 %all-to-all-start = ((bf16[3,128,3,4,192]{1,4,2,0,3:T(8,128)(2,1)}), bf16[3,128,3,4,192]{1,4,2,0,3:T(8,128)(2,1)}, u32[]{:S(2)}, u32[]{:S(2)}) async-start(bf16[3,128,3,4,192]{1,4,2,0,3:T(8,128)(2,1)} %copy.274), calls=%async_computation | async-start | bytes 3538944 | tf_op jit(solution)/shard_map/all_to_all | solution.py:84
  210.0 283.8 %copy-start.55 = (f32[2,128]{1,0:T(2,128)}, f32[2,128]{1,0:T(2,128)S(1)}, u32[]{:S(2)}) copy-start(f32[2,128]{1,0:T(2,128)S(1)} %broadcast_multiply_fusion.17) | copy-start | bytes 3076
  210.3 283.6 %copy-start.58 = (f32[2,128]{1,0:T(2,128)}, f32[2,128]{1,0:T(2,128)S(1)}, u32[]{:S(2)}) copy-start(f32[2,128]{1,0:T(2,128)S(1)} %add_rsqrt_fusion.4) | copy-start | bytes 3076
  382.6 19.2 %all-to-all-start.1 = ((bf16[3,512,1,192]{3,0,2,1:T(4,128)(2,1)}), bf16[3,512,1,192]{3,0,2,1:T(4,128)(2,1)}, u32[]{:S(2)}, u32[]{:S(2)}) async-start(bf16[3,512,1,192]{3,0,2,1:T(4,128)(2,1)} %copy.277), calls=%async_computation.1 | async-start | bytes 2097152 | tf_op jit(solution)/shard_map/all_to_all | solution.py:96
  407.9 107.2 %copy-start.53 = (f32[3,128]{1,0:T(4,128)}, f32[3,128]{1,0:T(4,128)S(1)}, u32[]{:S(2)}) copy-start(f32[3,128]{1,0:T(4,128)S(1)} %broadcast_multiply_fusion.7) | copy-start | bytes 4612
  408.2 107.0 %copy-start.57 = (f32[3,128]{1,0:T(4,128)}, f32[3,128]{1,0:T(4,128)S(1)}, u32[]{:S(2)}) copy-start(f32[3,128]{1,0:T(4,128)S(1)} %add_rsqrt_fusion.1) | copy-start | bytes 4612
  416.9 9.8 copy-start.13
  498.3 10.3 slice-start.13
  498.3 10.3 slice-start.15
  498.3 9.9 copy-start.14
  498.3 10.3 slice-start.14
  498.3 10.3 slice-start.16
  524.0 18.3 %all-to-all-start.2 = ((bf16[3,128,4,192]{1,3,0,2:T(8,128)(2,1)}), bf16[3,128,4,192]{1,3,0,2:T(8,128)(2,1)}, u32[]{:S(2)}, u32[]{:S(2)}) async-start(bf16[3,128,4,192]{1,3,0,2:T(8,128)(2,1)} %copy.290), calls=%async_computation.2 | async-start | bytes 1179648 | tf_op jit(solution)/shard_map/all_to_all | solution.py:111
  528.2 190.0 %reduce-scatter.12.cloned.1.call-start = ((), (), s32[]{:S(2)}) async-start(), calls=%async_computation.15 | async-start | bytes 2433024 | tf_op jit(solution)/shard_map/reduce_scatter | solution.py:204
  544.0 13.3 slice-start
  544.0 13.3 slice-start.1
  585.7 43.4 %all-to-all-start.3 = ((bf16[3,512,3,1,192]{4,2,0,3,1:T(4,128)(2,1)}), bf16[3,512,3,1,192]{4,2,0,3,1:T(4,128)(2,1)}, u32[]{:S(2)}, u32[]{:S(2)}) async-start(bf16[3,512,3,1,192]{4,2,0,3,1:T(4,128)(2,1)} %pad_maximum_fusion), calls=%async_computation.3 | async-start | bytes 6291456 | tf_op jit(solution)/shard_map/all_to_all | solution.py:123
  590.5 153.8 %reduce-scatter.18.cloned.1.call-start = ((), (), s32[]{:S(2)}) async-start(), calls=%async_computation.18 | async-start | bytes 1622016
  595.7 33.4 %copy-start.22 = (f32[2,128,768]{2,1,0:T(8,128)}, f32[2,128,768]{2,1,0:T(8,128)S(1)}, u32[]{:S(2)}) copy-start(f32[2,128,768]{2,1,0:T(8,128)S(1)} %fusion.124) | copy-start | bytes 2359300
  644.0 11.2 slice-start.3
  647.8 334.9 %all-reduce.7.cloned.1.call-start = ((), (), s32[]{:S(2)}) async-start(), calls=%async_computation.19 | async-start | bytes 25214976
  679.2 428.3 %reduce-scatter.10.cloned.1.call-start = ((), (), s32[]{:S(2)}) async-start(), calls=%async_computation.14 | async-start | bytes 7299072 | tf_op jit(solution)/shard_map/reduce_scatter | solution.py:203
  687.6 562.2 %reduce-scatter.16.cloned.1.call-start = ((), (), s32[]{:S(2)}) async-start(), calls=%async_computation.17 | async-start | bytes 9732096 | tf_op jit(solution)/shard_map/reduce_scatter | solution.py:206
  698.0 692.9 %reduce-scatter.14.cloned.1.call-start = ((), (), s32[]{:S(2)}) async-start(), calls=%async_computation.16 | async-start | bytes 9732096 | tf_op jit(solution)/shard_map/reduce_scatter | solution.py:205
  709.1 10.6 copy-start.102
  709.1 36.9 %copy-start.106 = (f32[24]{0:T(128)S(1)}, f32[24]{0:T(128)}, u32[]{:S(2)}) copy-start(f32[24]{0:T(128)} %param.46) | copy-start | bytes 292
  986.2 123.0 %copy-start.103 = (f32[24]{0:T(128)S(1)}, f32[24]{0:T(128)}, u32[]{:S(2)}) copy-start(f32[24]{0:T(128)} %param.47) | copy-start | bytes 292
  986.2 265.3 %copy-start.104 = (f32[96]{0:T(128)S(1)}, f32[96]{0:T(128)}, u32[]{:S(2)}) copy-start(f32[96]{0:T(128)} %param.53) | copy-start | bytes 1156
  987.6 471.7 %copy-start.46 = (f32[24,768]{1,0:T(8,128)S(1)}, f32[24,768]{1,0:T(8,128)}, u32[]{:S(2)}) copy-start(f32[24,768]{1,0:T(8,128)} %reduce-scatter.12.cloned.1.call-done) | copy-start | bytes 221188
  1107.5 351.0 %copy-start.37 = (f32[24,2304]{1,0:T(8,128)S(1)}, f32[24,2304]{1,0:T(8,128)}, u32[]{:S(2)}) copy-start(f32[24,2304]{1,0:T(8,128)} %reduce-scatter.10.cloned.1.call-done) | copy-start | bytes 663556
  1249.8 210.9 %copy-start.34 = (f32[96,768]{1,0:T(8,128)S(1)}, f32[96,768]{1,0:T(8,128)}, u32[]{:S(2)}) copy-start(f32[96,768]{1,0:T(8,128)} %reduce-scatter.16.cloned.1.call-done) | copy-start | bytes 884740
  1390.8 69.1 %copy-start.35 = (f32[24,3072]{1,0:T(8,128)S(1)}, f32[24,3072]{1,0:T(8,128)}, u32[]{:S(2)}) copy-start(f32[24,3072]{1,0:T(8,128)} %reduce-scatter.14.cloned.1.call-done) | copy-start | bytes 884740
  1444.0 82.2 %copy-start.52 = (f32[2304]{0:T(1024)}, f32[2304]{0:T(1024)S(1)}, u32[]{:S(2)}) copy-start(f32[2304]{0:T(1024)S(1)} %multiply_add_fusion.10) | copy-start | bytes 27652
  1446.1 81.7 %copy-start.51 = (f32[3072]{0:T(1024)}, f32[3072]{0:T(1024)S(1)}, u32[]{:S(2)}) copy-start(f32[3072]{0:T(1024)S(1)} %multiply_add_fusion.9) | copy-start | bytes 36868
  1449.4 65.0 %copy-start.50 = (f32[4101]{0:T(1024)}, f32[4101]{0:T(1024)S(1)}, u32[]{:S(2)}) copy-start(f32[4101]{0:T(1024)S(1)} %get-tuple-element.268) | copy-start | bytes 49216
  1514.4 11.1 copy-start.109
  1514.4 11.1 copy-start.108
  1514.4 11.1 copy-start.68
  1514.4 11.1 copy-start.69
  1514.4 11.1 copy-start.71
  1514.4 11.8 copy-start.45
  1514.4 11.8 copy-start.83
  1514.5 12.6 copy-start.47
  1514.5 12.6 copy-start.63
  1514.5 12.6 copy-start.80
  1514.5 13.3 copy-start.42
  1514.5 13.3 copy-start.78
  1517.6 11.0 copy-start.44
  1517.6 11.0 copy-start.61
  1517.6 11.0 copy-start.76
  (78 other events, 394.7 us)
Sparse Core Ops, SparseCore 0:
  11.5 76.5 all-gather.6
  91.6 59.1 all-gather.8
  154.3 53.5 all-gather.10
  211.2 62.5 all-gather.12
  277.2 62.4 all-gather.14
  537.6 99.6 reduce-scatter.11
  648.0 96.3 reduce-scatter.17
  751.7 231.0 all-reduce.6
  989.0 118.4 reduce-scatter.9
  1114.8 134.9 reduce-scatter.15
  1256.2 134.5 reduce-scatter.13
where the time goes:
time: 1550 us; the launch traced here: 1540 us
  waiting for transfers between devices  886 us (57%)
  blocking collectives  206 us (13%)
  matrix products  176 us (11%)
  local copies, waits for them, and re-layouts  114 us (7%)
  other arithmetic  103 us (7%)
  between operations  32 us (2%)
  starting transfers between devices  19.2 us (1%)
    unnamed x13, waiting for transfers between devices  260 us
    reduce_scatter x1, waiting for transfers between devices, reduce_once(): lax.psum_scatter(grads[5], ('dp', 'seq'), scatter_dimension=0, tiled=True)  140 us
    reduce_scatter x1, waiting for transfers between devices, reduce_once(): lax.psum_scatter(grads[4], ('dp', 'seq'), scatter_dimension=0, tiled=True)  138 us
    reduce_scatter x1, waiting for transfers between devices, reduce_once(): lax.psum_scatter(grads[2], ('dp', 'seq'), scatter_dimension=0, tiled=True)  119 us
    all_gather x1, waiting for transfers between devices, on_device(): lax.all_gather(in_weight.astype(jnp.bfloat16), ('dp', 'seq'), axis=0, til...  63.6 us
    all_gather x1, waiting for transfers between devices, on_device(): lax.all_gather(down_weight.astype(jnp.bfloat16), ('dp', 'seq'), axis=0, t...  60.3 us
    all_gather x1, blocking collectives, on_device(): lax.all_gather(norms.astype(jnp.bfloat16), ('dp', 'seq'), axis=0, tiled=T...  43.7 us
    unnamed x1, blocking collectives  42.5 us
  transfers between devices with their start and end apart: 15, of which 11 were waited for; matrix products, arithmetic and copies ran while one was open for 16% of the time, Pallas kernels for 0%

commit v1 on v0

v1 whole, which is shorter than its diff:
```python
import functools

import jax
import jax.numpy as jnp
from jax import lax
from jax.experimental import pallas as pl
from jax.experimental.pallas import tpu as pltpu
from jax.sharding import PartitionSpec as P

D = 768
HEADS = 12
HEAD_DIM = 64
VOCAB = 4101
STEP = 10
SPAN = 128

EPSILON = 1e-12
SQUARE_FLOOR = 1e-30
learn_rate = 0.3

MESH = pl.DeviceIdType.MESH
F32 = jnp.float32
BF16 = jnp.bfloat16

NORM_AT = VOCAB
COUNT_AT = VOCAB + 6
PLACE_AT = 4352
WIDE = PLACE_AT + 512

SHAPES = ((24, WIDE), (24, 3 * D), (24, D), (24, 4 * D), (96, D))
E_, Q_, O_, I_, D_ = range(5)
CLASS_A, CLASS_B, CLASS_C = (E_, O_), (Q_, D_), (I_,)
UP, DOWN, XWAY, YWAY, SIDE = range(5)


def here():
    dp, seq = lax.axis_index("dp"), lax.axis_index("seq")
    return dp // 2, dp % 2, seq // 2, seq % 2


def device(z, y, x, c):
    return {"dp": z * 2 + y, "seq": x * 2 + c}


def chip(z, y, x):
    return z * 4 + y * 2 + x


def near_first(z, s):
    inner = (z * (3 - z)) // 2
    found = s + inner * (1, 1, -2, 0)[s]
    return found + (z // 2) * (3 - 2 * found)


def greet(peers):
    barrier = pltpu.get_barrier_semaphore()
    z, y, x, c = here()

    @pl.when(z < 3)
    def _():
        pl.semaphore_signal(barrier, inc=1, device_id=peers[UP], device_id_type=MESH)

    @pl.when(z > 0)
    def _():
        pl.semaphore_signal(barrier, inc=1, device_id=peers[DOWN], device_id_type=MESH)

    for way in (XWAY, YWAY, SIDE):
        pl.semaphore_signal(barrier, inc=1, device_id=peers[way], device_id_type=MESH)

    @pl.when((z == 0) | (z == 3))
    def _():
        pl.semaphore_wait(barrier, 4)

    @pl.when((z > 0) & (z < 3))
    def _():
        pl.semaphore_wait(barrier, 5)


def all_peers():
    z, y, x, c = here()
    return (
        device(z + 1, y, x, c),
        device(z - 1, y, x, c),
        device(z, y, 1 - x, c),
        device(z, 1 - y, x, c),
        device(z, y, x, 1 - c),
    )


def gather_kernel(*refs):
    shards, outs, merge, mine = refs[0:5], refs[5:10], refs[10:15], refs[15:20]
    swap_send, swap_recv, local_sem, send_sem, link_recv, side_recv = refs[20:]
    z, y, x, c = here()
    peers = all_peers()
    me = chip(z, y, x)

    def part(m, k, half):
        size, wide = 2 * SHAPES[m][0], SHAPES[m][1] // 2
        return outs[m].at[
            pl.ds(pl.multiple_of(k * size, size), size), pl.ds(pl.multiple_of(half * wide, 128), wide)
        ]

    def copy_of(m, k, way, own):
        return pltpu.make_async_remote_copy(
            src_ref=mine[m] if own else part(m, k, c),
            dst_ref=part(m, k, c),
            send_sem=send_sem.at[m, k, way],
            recv_sem=(side_recv if way == SIDE else link_recv).at[m, k],
            device_id=peers[way],
            device_id_type=MESH,
        )

    sent = []

    def push(m, k, way, own=False, only=None):
        sent.append((m, k, way, own, only))
        if only is None:
            copy_of(m, k, way, own).start()
        else:

            @pl.when(only)
            def _():
                copy_of(m, k, way, own).start()

    def arrived(m, k):
        copy_of(m, k, XWAY, False).wait_recv()

    greet(peers)
    swaps = []
    for m, (size, wide) in enumerate(SHAPES):
        half = wide // 2
        swaps.append(
            pltpu.make_async_remote_copy(
                src_ref=shards[m].at[:, pl.ds(pl.multiple_of((1 - c) * half, 128), half)],
                dst_ref=merge[m].at[pl.ds(pl.multiple_of(c * size, 8), size), :],
                send_sem=swap_send.at[m],
                recv_sem=swap_recv.at[m],
                device_id=peers[SIDE],
                device_id_type=MESH,
            )
        )
        swaps[m].start()
    for m, (size, wide) in enumerate(SHAPES):
        half = wide // 2
        merge[m][pl.ds(pl.multiple_of(c * size, 8), size), :] = shards[m][
            :, pl.ds(pl.multiple_of(c * half, 128), half)
        ]

    keeps = []
    for m in (I_, E_, Q_, D_, O_):
        swaps[m].wait_recv()
        mine[m][...] = merge[m][...].astype(BF16)
        for way, only in ((UP, z < 3), (DOWN, z > 0), (XWAY, None), (YWAY, None), (SIDE, None)):
            push(m, me, way, True, only)
        keeps.append(pltpu.make_async_copy(mine[m], part(m, me, c), local_sem.at[m]))
        keeps[-1].start()

    def onward(m, k, far):
        push(m, k, UP, only=(far < z) & (z < 3))
        push(m, k, DOWN, only=(far > z) & (z > 0))

    def line(ms, s, ways):
        far = near_first(z, s)
        k = chip(far, y, x)
        for m in ms:
            arrived(m, k)
            onward(m, k, far)
            for way in ways:
                push(m, k, way)

    def second(ms, s, axis):
        far = near_first(z, s)
        k = chip(far, y, 1 - x) if axis == XWAY else chip(far, 1 - y, x)
        for m in ms:
            arrived(m, k)
            push(m, k, YWAY if axis == XWAY else XWAY)
            push(m, k, SIDE)

    def third(ms, s, axis):
        far = near_first(z, s)
        for other in range(2):
            k = chip(far, 1 - y, other) if axis == YWAY else chip(far, other, 1 - x)
            for m in ms:
                arrived(m, k)
                push(m, k, SIDE)

    def c_first():
        k = chip(z, 1 - y, x)
        for m in CLASS_C:
            arrived(m, k)
            push(m, k, XWAY)
            push(m, k, UP, only=z < 3)
            push(m, k, DOWN, only=z > 0)
            push(m, k, SIDE)

    def c_second():
        for other in (y, 1 - y):
            k = chip(z, other, 1 - x)
            for m in CLASS_C:
                arrived(m, k)
                push(m, k, UP, only=z < 3)
                push(m, k, DOWN, only=z > 0)
                push(m, k, SIDE)

    def c_line(s):
        far = near_first(z, s)
        for k in (chip(far, y, x), chip(far, 1 - y, x), chip(far, y, 1 - x), chip(far, 1 - y, 1 - x)):
            for m in CLASS_C:
                arrived(m, k)
                onward(m, k, far)
                push(m, k, SIDE)

    both = (XWAY, YWAY, SIDE)
    c_first()
    line(CLASS_A, 1, both)
    line(CLASS_B, 1, both)
    c_second()
    second(CLASS_A, 0, XWAY)
    second(CLASS_B, 0, YWAY)
    c_line(1)
    line(CLASS_A, 2, both)
    line(CLASS_B, 2, both)
    second(CLASS_A, 1, XWAY)
    second(CLASS_B, 1, YWAY)
    c_line(2)
    line(CLASS_A, 3, both)
    line(CLASS_B, 3, both)
    second(CLASS_A, 2, XWAY)
    second(CLASS_B, 2, YWAY)
    c_line(3)
    second(CLASS_A, 3, XWAY)
    second(CLASS_B, 3, YWAY)
    for s in range(4):
        third(CLASS_A, s, YWAY)
        third(CLASS_B, s, XWAY)
    for m in range(5):
        for k in range(16):
            pltpu.make_async_remote_copy(
                src_ref=part(m, k, 1 - c),
                dst_ref=part(m, k, 1 - c),
                send_sem=send_sem.at[m, k, SIDE],
                recv_sem=side_recv.at[m, k],
                device_id=peers[SIDE],
                device_id_type=MESH,
            ).wait_recv()
    for swap in swaps:
        swap.wait_send()
    for keep in keeps:
        keep.wait()
    for m, k, way, own, only in sent:
        if only is None:
            copy_of(m, k, way, own).wait_send()
        else:

            @pl.when(only)
            def _(m=m, k=k, way=way, own=own):
                copy_of(m, k, way, own).wait_send()


def gather_weights(shards):
    return pl.pallas_call(
        gather_kernel,
        out_shape=[jax.ShapeDtypeStruct((32 * size, wide), BF16) for size, wide in SHAPES],
        in_specs=[pl.BlockSpec(memory_space=pltpu.VMEM)] * 5,
        out_specs=[pl.BlockSpec(memory_space=pl.ANY)] * 5,
        scratch_shapes=[pltpu.VMEM((2 * size, wide // 2), F32) for size, wide in SHAPES]
        + [pltpu.VMEM((2 * size, wide // 2), BF16) for size, wide in SHAPES]
        + [
            pltpu.SemaphoreType.DMA((5,)),
            pltpu.SemaphoreType.DMA((5,)),
            pltpu.SemaphoreType.DMA((5,)),
            pltpu.SemaphoreType.DMA((5, 16, 5)),
            pltpu.SemaphoreType.DMA((5, 16)),
            pltpu.SemaphoreType.DMA((5, 16)),
        ],
        compiler_params=pltpu.CompilerParams(
            collective_id=0, has_side_effects=True, vmem_limit_bytes=48 * 1024 * 1024
        ),
    )(*shards)


def reduce_kernel(*refs):
    grads, outs = refs[0:5], refs[5:10]
    own, side, first, second, low, high, fin = (refs[10 + 5 * i : 15 + 5 * i] for i in range(7))
    own_sem, side_send, side_recv, first_send, first_recv, second_send, second_recv = refs[45:52]
    up_send, low_recv, down_send, high_recv, swap_send, swap_recv = refs[52:]
    z, y, x, c = here()
    peers = all_peers()
    me = chip(z, y, x)

    def slot(ref, m, index):
        size = 2 * SHAPES[m][0]
        return ref[m].at[pl.ds(pl.multiple_of(index * size, size), size), :]

    def cols(m, half):
        wide = SHAPES[m][1] // 2
        return pl.ds(pl.multiple_of(half * wide, 128), wide)

    def combine(m, target, parts):
        def step(j, carry):
            at = pl.ds(pl.multiple_of(j * 128, 128), 128)
            total = parts[0][:, at].astype(F32)
            for member in parts[1:]:
                total = total + member[:, at].astype(F32)
            target[:, at] = total.astype(target.dtype)
            return carry

        lax.fori_loop(0, SHAPES[m][1] // 256, step, 0)

    def side_copy(m, k):
        size = 2 * SHAPES[m][0]
        return pltpu.make_async_remote_copy(
            src_ref=grads[m].at[pl.ds(pl.multiple_of(k * size, size), size), cols(m, 1 - c)],
            dst_ref=slot(side, m, k),
            send_sem=side_send.at[m, k],
            recv_sem=side_recv.at[m, k],
            device_id=peers[SIDE],
            device_id_type=MESH,
        )

    def own_copy(m):
        return pltpu.make_async_copy(grads[m].at[:, cols(m, c)], own[m], own_sem.at[m])

    def hop(m, k, land, index, sems, way):
        return pltpu.make_async_remote_copy(
            src_ref=slot(own, m, k),
            dst_ref=slot(land, m, index),
            send_sem=sems[0].at[m, index],
            recv_sem=sems[1].at[m, index],
            device_id=peers[way],
            device_id_type=MESH,
        )

    FIRST, SECOND = (first_send, first_recv), (second_send, second_recv)
    RISE, FALL = (up_send, low_recv), (down_send, high_recv)
    sent = []

    def send(m, k, land, index, sems, way, only=None):
        sent.append((m, k, land, index, sems, way, only))
        hop(m, k, land, index, sems, way).start()

    def landed(m, land, index, sems):
        hop(m, me, land, index, sems, XWAY).wait_recv()

    def block(m, a, b, far):
        return chip(far, a, b) if m in CLASS_A else chip(far, b, a)

    def split(m):
        return (y, x, YWAY, XWAY) if m in CLASS_A else (x, y, XWAY, YWAY)

    greet(peers)
    for m in (E_, Q_, I_, D_, O_):
        own_copy(m).start()

    def side_order():
        for i in range(8):
            for m in CLASS_A + CLASS_B:
                a, b, _, _ = split(m)
                yield m, block(m, 1 - a, i % 2, i // 2)
            for m in CLASS_C:
                for n in range(2):
                    yield m, (z * 4 + 4 + 2 * i + n) % 16
        for i in range(8):
            for m in CLASS_A + CLASS_B:
                a, b, _, _ = split(m)
                other = 1 - b if i < 4 else b
                yield m, block(m, a, other, i % 4)

    order = list(side_order())
    for m, k in order:
        side_copy(m, k).start()

    loaded = set()

    def ready(m, k):
        if m not in loaded:
            loaded.add(m)
            own_copy(m).wait()
        side_copy(m, k).wait_recv()

    def c_rise(t, yx):
        k = t * 4 + yx
        below = z < t
        for m in CLASS_C:

            @pl.when(below)
            def _():
                side_copy(m, k).wait_recv()

                @pl.when(z == 0)
                def _():
                    combine(m, slot(own, m, k), (slot(own, m, k), slot(side, m, k)))

                @pl.when(z > 0)
                def _():
                    landed(m, low, k, RISE)
                    combine(m, slot(own, m, k), (slot(own, m, k), slot(side, m, k), slot(low, m, k)))

                send(m, k, low, k, RISE, UP, below)

    def c_fall(t, yx):
        k = t * 4 + yx
        above = z > t
        for m in CLASS_C:

            @pl.when(above)
            def _():
                side_copy(m, k).wait_recv()

                @pl.when(z == 3)
                def _():
                    combine(m, slot(own, m, k), (slot(own, m, k), slot(side, m, k)))

                @pl.when(z < 3)
                def _():
                    landed(m, high, k, FALL)
                    combine(m, slot(own, m, k), (slot(own, m, k), slot(side, m, k), slot(high, m, k)))

                send(m, k, high, k, FALL, DOWN, above)

    c_steps = []
    for t in range(3):
        for yx in range(4):
            c_steps.append((c_rise, 3 - t, yx))
            c_steps.append((c_fall, t, yx))

    for m in CLASS_C:
        loaded.add(m)
        own_copy(m).wait()
    for i in range(8):
        for m in CLASS_A + CLASS_B:
            a, b, way, _ = split(m)
            k = block(m, 1 - a, i % 2, i // 2)
            ready(m, k)
            combine(m, slot(own, m, k), (slot(own, m, k), slot(side, m, k)))
            send(m, k, first, i, FIRST, way)
        for call, t, yx in c_steps[3 * i : 3 * i + 3]:
            call(t, yx)

    for i in range(4):
        for m in CLASS_A + CLASS_B:
            a, b, _, way = split(m)
            k = block(m, a, 1 - b, i)
            ready(m, k)
            at = 2 * i + (1 - b)
            landed(m, first, at, FIRST)
            combine(m, slot(own, m, k), (slot(own, m, k), slot(side, m, k), slot(first, m, at)))
            send(m, k, second, i, SECOND, way)
        if i == 0:
            for m in CLASS_C:
                for other in range(2):
                    k = chip(z, other, 1 - x)
                    ready(m, k)

                    @pl.when(z > 0)
                    def _():
                        landed(m, low, k, RISE)

                    @pl.when(z < 3)
                    def _():
                        landed(m, high, k, FALL)

                    with_ends(z, m, k, slot, own, side, low, high, combine, slot(own, m, k), ())
                    send(m, k, first, other, FIRST, XWAY)
        if i == 2:
            for m in CLASS_C:
                k = chip(z, 1 - y, x)
                ready(m, k)

                @pl.when(z > 0)
                def _():
                    landed(m, low, k, RISE)

                @pl.when(z < 3)
                def _():
                    landed(m, high, k, FALL)

                landed(m, first, 1 - y, FIRST)
                with_ends(
                    z, m, k, slot, own, side, low, high, combine, slot(own, m, k), (slot(first, m, 1 - y),)
                )
                send(m, k, second, 0, SECOND, YWAY)

    def z_parts(m, t):
        a, b, _, _ = split(m)
        k = block(m, a, b, t)
        return k, (slot(own, m, k), slot(side, m, k), slot(first, m, 2 * t + b), slot(second, m, t))

    def z_ready(m, k, t):
        a, b, _, _ = split(m)
        side_copy(m, k).wait_recv()
        landed(m, first, 2 * t + b, FIRST)
        landed(m, second, t, SECOND)

    for step in range(3):
        t = 3 - step
        below = z < t
        for m in CLASS_A + CLASS_B:
            k, parts = z_parts(m, t)

            @pl.when(below)
            def _():
                z_ready(m, k, t)

                @pl.when(z == 0)
                def _():
                    combine(m, slot(own, m, k), parts)

                @pl.when(z > 0)
                def _():
                    landed(m, low, t, RISE)
                    combine(m, slot(own, m, k), parts + (slot(low, m, t),))

                send(m, k, low, t, RISE, UP, below)

        t = step
        above = z > t
        for m in CLASS_A + CLASS_B:
            k, parts = z_parts(m, t)

            @pl.when(above)
            def _():
                z_ready(m, k, t)

                @pl.when(z == 3)
                def _():
                    combine(m, slot(own, m, k), parts)

                @pl.when(z < 3)
                def _():
                    landed(m, high, t, FALL)
                    combine(m, slot(own, m, k), parts + (slot(high, m, t),))

                send(m, k, high, t, FALL, DOWN, above)

    swaps = []
    for m in CLASS_C + CLASS_A + CLASS_B:
        if m in CLASS_C:
            ready(m, me)
            landed(m, first, y, FIRST)
            landed(m, second, 0, SECOND)
            at, more = me, (slot(first, m, y), slot(second, m, 0))
        else:
            z_ready(m, me, z)
            at, more = z, z_parts(m, z)[1][2:]

        @pl.when(z > 0)
        def _():
            landed(m, low, at, RISE)

        @pl.when(z < 3)
        def _():
            landed(m, high, at, FALL)

        with_ends(z, m, me, slot, own, side, low, high, combine, fin[m], more, at)
        size = SHAPES[m][0]
        swaps.append(
            pltpu.make_async_remote_copy(
                src_ref=fin[m].at[pl.ds(pl.multiple_of((1 - c) * size, 8), size), :],
                dst_ref=outs[m].at[:, cols(m, c)],
                send_sem=swap_send.at[m],
                recv_sem=swap_recv.at[m],
                device_id=peers[SIDE],
                device_id_type=MESH,
            )
        )
        swaps[-1].start()
        outs[m][:, cols(m, c)] = fin[m][pl.ds(pl.multiple_of(c * size, 8), size), :]
    for swap in swaps:
        swap.wait()
    for m, k in order:
        side_copy(m, k).wait_send()
    for m, k, land, index, sems, way, only in sent:
        if only is None:
            hop(m, k, land, index, sems, way).wait_send()
        else:

            @pl.when(only)
            def _(m=m, k=k, land=land, index=index, sems=sems, way=way):
                hop(m, k, land, index, sems, way).wait_send()


def with_ends(z, m, k, slot, own, side, low, high, combine, target, more, at=None):
    at = k if at is None else at
    base = (slot(own, m, k), slot(side, m, k)) + more

    @pl.when(z == 0)
    def _():
        combine(m, target, base + (slot(high, m, at),))

    @pl.when(z == 3)
    def _():
        combine(m, target, base + (slot(low, m, at),))

    @pl.when((z > 0) & (z < 3))
    def _():
        combine(m, target, base + (slot(low, m, at), slot(high, m, at)))


def reduce_grads(grads):
    def rows(count, m):
        size, wide = SHAPES[m]
        return pltpu.VMEM((count * 2 * size, wide // 2), BF16)

    every = range(5)
    scratch = (
        [rows(16, m) for m in every]
        + [rows(16, m) for m in every]
        + [rows(2 if m in CLASS_C else 8, m) for m in every]
        + [rows(1 if m in CLASS_C else 4, m) for m in every]
        + [rows(16 if m in CLASS_C else 4, m) for m in every]
        + [rows(16 if m in CLASS_C else 4, m) for m in every]
        + [pltpu.VMEM((2 * size, wide // 2), F32) for size, wide in SHAPES]
        + [pltpu.SemaphoreType.DMA((5,))]
        + [pltpu.SemaphoreType.DMA((5, 16))] * 2
        + [pltpu.SemaphoreType.DMA((5, 8))] * 2
        + [pltpu.SemaphoreType.DMA((5, 4))] * 2
        + [pltpu.SemaphoreType.DMA((5, 16))] * 4
        + [pltpu.SemaphoreType.DMA((5,))] * 2
    )
    return pl.pallas_call(
        reduce_kernel,
        out_shape=[jax.ShapeDtypeStruct(shape, F32) for shape in SHAPES],
        in_specs=[pl.BlockSpec(memory_space=pl.ANY)] * 5,
        out_specs=[pl.BlockSpec(memory_space=pltpu.VMEM)] * 5,
        scratch_shapes=scratch,
        compiler_params=pltpu.CompilerParams(
            collective_id=1, has_side_effects=True, vmem_limit_bytes=56 * 1024 * 1024
        ),
    )(*grads)


def total_kernel(in_ref, out_ref, land, held, send_sem, recv_sem):
    z, y, x, c = here()
    near = z + 1 - 2 * (z % 2)
    far = (z + 2) % 4
    partners = (
        device(z, y, x, 1 - c),
        device(z, y, 1 - x, c),
        device(z, 1 - y, x, c),
        device(near, y, x, c),
        device(far, y, x, c),
    )
    barrier = pltpu.get_barrier_semaphore()
    for partner in partners:
        pl.semaphore_signal(barrier, inc=1, device_id=partner, device_id_type=MESH)
    pl.semaphore_wait(barrier, 5)
    held[0] = in_ref[...]
    copies = []
    for i, partner in enumerate(partners):
        copies.append(
            pltpu.make_async_remote_copy(
                src_ref=held.at[i],
                dst_ref=land.at[i],
                send_sem=send_sem.at[i],
                recv_sem=recv_sem.at[i],
                device_id=partner,
                device_id_type=MESH,
            )
        )
        copies[i].start()
        copies[i].wait_recv()
        held[i + 1] = held[i] + land[i]
    out_ref[...] = held[5]
    for copy in copies:
        copy.wait_send()


def total_of(array, collective_id):
    return pl.pallas_call(
        total_kernel,
        out_shape=jax.ShapeDtypeStruct(array.shape, F32),
        in_specs=[pl.BlockSpec(memory_space=pltpu.VMEM)],
        out_specs=pl.BlockSpec(memory_space=pltpu.VMEM),
        scratch_shapes=[
            pltpu.VMEM((5,) + array.shape, F32),
            pltpu.VMEM((6,) + array.shape, F32),
            pltpu.SemaphoreType.DMA((5,)),
            pltpu.SemaphoreType.DMA((5,)),
        ],
        compiler_params=pltpu.CompilerParams(collective_id=collective_id, has_side_effects=True),
    )(array)


def gelu_pair(hidden):
    normal_cdf = 0.5 * (1.0 + lax.erf(hidden * 0.7071067811865476))
    return (
        hidden * normal_cdf,
        normal_cdf + hidden * jnp.exp(-0.5 * hidden * hidden) * 0.3989422804014327,
    )


def norm_forward(value, gain, shift):
    centred = value - jnp.mean(value, -1, keepdims=True)
    inverse = lax.rsqrt(jnp.mean(centred * centred, -1, keepdims=True) + EPSILON)
    normed = centred * inverse
    return (normed * gain + shift, normed, inverse)


def norm_backward(grad_out, normed, inverse, gain):
    scaled = grad_out * gain
    back = inverse * (
        scaled
        - jnp.mean(scaled, -1, keepdims=True)
        - normed * jnp.mean(scaled * normed, -1, keepdims=True)
    )
    return (back, jnp.sum(grad_out * normed, 0), jnp.sum(grad_out, 0))


def mm(left, right, sides):
    return lax.dot_general(left, right, ((sides[:1], sides[1:]), ((), ())), preferred_element_type=F32)


def attend(qkv, allowed):
    by_head = qkv.reshape(qkv.shape[0], 3, HEADS, HEAD_DIM)
    query, key, value = by_head[:, 0], by_head[:, 1], by_head[:, 2]
    scores = jnp.einsum("qhe,khe->hqk", query, key, preferred_element_type=F32) * 0.125
    scores = jnp.where(allowed[None], scores, -1e30)
    highest = jnp.max(scores, -1, keepdims=True)
    raised = jnp.exp(scores - highest)
    summed = jnp.sum(raised, -1, keepdims=True)
    shares = (raised / summed).astype(BF16)
    mixture = jnp.einsum("hqk,khe->qhe", shares, value, preferred_element_type=F32)
    return mixture.astype(BF16).reshape(qkv.shape[0], D), highest + jnp.log(summed)


def attend_back(qkv, allowed, log_total, grad_mix):
    by_head = qkv.reshape(qkv.shape[0], 3, HEADS, HEAD_DIM)
    query, key, value = by_head[:, 0], by_head[:, 1], by_head[:, 2]
    grad_mix = grad_mix.reshape(qkv.shape[0], HEADS, HEAD_DIM)
    scores = jnp.einsum("qhe,khe->hqk", query, key, preferred_element_type=F32) * 0.125
    scores = jnp.where(allowed[None], scores, -1e30)
    shares = jnp.exp(scores - log_total)
    grad_share = jnp.einsum("qhe,khe->hqk", grad_mix, value, preferred_element_type=F32)
    grad_score = (shares * (grad_share - jnp.sum(shares * grad_share, -1, keepdims=True))).astype(BF16)
    grad_query = jnp.einsum("hqk,khe->qhe", grad_score, key, preferred_element_type=F32) * 0.125
    grad_key = jnp.einsum("hqk,qhe->khe", grad_score, query, preferred_element_type=F32) * 0.125
    grad_value = jnp.einsum("hqk,qhe->khe", shares.astype(BF16), grad_mix, preferred_element_type=F32)
    return jnp.stack((grad_query, grad_key, grad_value), 1).astype(BF16).reshape(qkv.shape)


def on_device(
    whole_mesh,
    long_ids,
    long_targets,
    long_mask,
    long_lengths,
    short_ids,
    short_targets,
    short_mask,
    short_lengths,
    table,
    position,
    qkv_weight,
    out_weight,
    in_weight,
    down_weight,
    norms,
    table_rows,
    table_cols,
    position_rows,
    position_cols,
    qkv_rows,
    qkv_cols,
    out_rows,
    out_cols,
    in_rows,
    in_cols,
    down_rows,
    down_cols,
    norm_moment,
):
    devices = lax.axis_size(("dp", "seq"))
    fast = whole_mesh == (8, 4)
    seq_index = lax.axis_index("seq")
    held = norms.shape[0]

    span = long_ids.shape[1]
    long_place = seq_index * span + lax.iota(jnp.int32, span)
    long_keep = (long_place[None, :] < long_lengths[:, None]).astype(jnp.int32)
    short_keep = (lax.iota(jnp.int32, SPAN)[None, :] < short_lengths[:, None]).astype(jnp.int32)
    long_pack = jnp.stack((long_ids, long_targets, long_mask * long_keep, long_keep), 1)
    short_pack = jnp.stack((short_ids, short_targets, short_mask * short_keep, short_keep), 1)
    moved = lax.all_to_all(
        jnp.concatenate((long_pack, short_pack[1:]), 0), "seq", split_axis=0, concat_axis=0, tiled=True
    )
    tokens = jnp.concatenate((moved, short_pack[:1]), 0)
    ids, targets, weight, keep = (tokens[:, i].reshape(-1) for i in range(4))
    weight = weight.astype(F32)
    count = tokens.shape[0] * span
    last = count - span
    alone = seq_index == lax.axis_size("seq") - 1
    token = lax.iota(jnp.int32, count)
    place = jnp.where(alone | (token >= last), token % span, token)
    row = jnp.where(alone | (token >= last), token // span, 0)
    allowed_long = (row[:last, None] == row[None, :last]) & (keep[None, :last] > 0)
    allowed_short = jnp.broadcast_to(keep[None, last:] > 0, (span, span))

    here_count = jnp.sum(long_pack[:, 2]) + jnp.sum(short_pack[:, 2])
    tall = table.T
    counts = jnp.broadcast_to(jnp.stack((here_count // 256, here_count % 256)).astype(F32)[None], (held, 2))
    wide_shard = jnp.concatenate(
        (tall, norms, counts, jnp.zeros((held, PLACE_AT - COUNT_AT - 2), F32), position.T), 1
    )
    shards = (wide_shard, qkv_weight, out_weight, in_weight, down_weight)
    if fast:
        wide_w, qkv_w, out_w, in_w, down_w = gather_weights(shards)
    else:
        wide_w, qkv_w, out_w, in_w, down_w = (
            lax.all_gather(shard.astype(BF16), ("dp", "seq"), axis=0, tiled=True) for shard in shards
        )
    gains = wide_w[:, NORM_AT : NORM_AT + 6].astype(F32)
    sums = jnp.sum(wide_w[:, COUNT_AT : COUNT_AT + 2].astype(F32), 0)
    mask_count = (sums[0] * 256.0 + sums[1]) / held
    inverse_count = 1.0 / mask_count

    column = lax.broadcasted_iota(jnp.int32, (1, WIDE), 1)
    chosen = ((ids[:, None] == column) | ((place[:, None] + PLACE_AT) == column)).astype(BF16)
    embedded = mm(chosen, wide_w, (1, 1))
    first, normed_a, inverse_a = norm_forward(embedded, gains[:, 0], gains[:, 1])
    first_b = first.astype(BF16)
    qkv_b = mm(first_b, qkv_w, (1, 0)).astype(BF16)
    mix_long, total_long = attend(qkv_b[:last], allowed_long)
    mix_short, total_short = attend(qkv_b[last:], allowed_short)
    mixture = jnp.concatenate((mix_long, mix_short), 0)
    second, normed_b, inverse_b = norm_forward(first + mm(mixture, out_w, (1, 0)), gains[:, 2], gains[:, 3])
    second_b = second.astype(BF16)
    hidden = mm(second_b, in_w, (1, 0))
    active, slope = gelu_pair(hidden)
    active_b = active.astype(BF16)
    third, normed_c, inverse_c = norm_forward(second + mm(active_b, down_w, (1, 0)), gains[:, 4], gains[:, 5])
    third_b = third.astype(BF16)
    logits = jnp.where(column < VOCAB, mm(third_b, wide_w, (1, 0)), -1e30)
    highest = jnp.max(logits, -1, keepdims=True)
    log_sum = highest + jnp.log(jnp.sum(jnp.exp(logits - highest), -1, keepdims=True))
    onehot = targets[:, None] == column
    picked = jnp.sum(jnp.where(onehot, logits, 0.0), -1)
    loss_part = jnp.sum(weight * (log_sum[:, 0] - picked))
    grad_logit = (
        (jnp.exp(logits - log_sum) - onehot.astype(F32)) * (weight * inverse_count)[:, None]
    ).astype(BF16)
    grad_third = mm(grad_logit, wide_w, (1, 1))
    grad_second, gain_c, shift_c = norm_backward(grad_third, normed_c, inverse_c, gains[:, 4])
    grad_ffn = grad_second.astype(BF16)
    down_grad = mm(active_b, grad_ffn, (0, 0)).astype(BF16)
    grad_hidden = (mm(grad_ffn, down_w, (1, 1)) * slope).astype(BF16)
    in_grad = mm(second_b, grad_hidden, (0, 0)).astype(BF16)
    grad_second = grad_second + mm(grad_hidden, in_w, (1, 1))
    grad_first, gain_b, shift_b = norm_backward(grad_second, normed_b, inverse_b, gains[:, 2])
    grad_attn = grad_first.astype(BF16)
    out_grad = mm(mixture, grad_attn, (0, 0)).astype(BF16)
    grad_mix = mm(grad_attn, out_w, (1, 1)).astype(BF16)
    grad_qkv = jnp.concatenate(
        (
            attend_back(qkv_b[:last], allowed_long, total_long, grad_mix[:last]),
            attend_back(qkv_b[last:], allowed_short, total_short, grad_mix[last:]),
        ),
        0,
    )
    qkv_grad = mm(first_b, grad_qkv, (0, 0)).astype(BF16)
    grad_first = grad_first + mm(grad_qkv, qkv_w, (1, 1))
    grad_embed, gain_a, shift_a = norm_backward(grad_first, normed_a, inverse_a, gains[:, 0])
    wide_grad = mm(
        jnp.concatenate((third_b, grad_embed.astype(BF16)), 0),
        jnp.concatenate((grad_logit, chosen), 0),
        (0, 0),
    )
    norm_part = jnp.stack((gain_a, shift_a, gain_b, shift_b, gain_c, shift_c), 1)
    wide_grad = lax.dynamic_update_slice(wide_grad.astype(BF16), norm_part.astype(BF16), (0, NORM_AT))
    grads = (wide_grad, qkv_grad, out_grad, in_grad, down_grad)
    if fast:
        wide_g, qkv_g, out_g, in_g, down_g = reduce_grads(grads)
    else:
        wide_g, qkv_g, out_g, in_g, down_g = (
            lax.psum_scatter(grad.astype(F32), ("dp", "seq"), scatter_dimension=0, tiled=True) for grad in grads
        )
    table_g, place_g = wide_g[:, :VOCAB], wide_g[:, PLACE_AT:]
    norm_g = wide_g[:, NORM_AT : NORM_AT + 6]

    def summed_over_all(parts, collective_id):
        if not fast:
            return lax.psum(parts, ("dp", "seq"))
        flat = jnp.concatenate([member.reshape(-1) for member in parts])
        room = -flat.shape[0] % 1024
        flat = jnp.concatenate((flat, jnp.zeros((room,), F32))).reshape(-1, 128)
        flat = total_of(flat, collective_id).reshape(-1)
        found, start = [], 0
        for member in parts:
            found.append(flat[start : start + member.size].reshape(member.shape))
            start += member.size
        return found

    decay = 1.0 - STEP ** (-0.8)
    matrices = (
        (qkv_weight, qkv_g, qkv_rows, qkv_cols),
        (out_weight, out_g, out_rows, out_cols),
        (in_weight, in_g, in_rows, in_cols),
        (down_weight, down_g, down_rows, down_cols),
    )
    wide = (
        (tall, table_g, table_cols, table_rows),
        (position.T, place_g, position_cols, position_rows),
    )
    row_news = [
        decay * member[2] + (1.0 - decay) * jnp.mean(member[1] * member[1] + SQUARE_FLOOR, 1)
        for member in matrices + wide
    ]
    col_parts = [jnp.sum(member[1] * member[1] + SQUARE_FLOOR, 0) for member in matrices + wide]
    row_totals = jnp.stack([jnp.sum(rows_new) for rows_new in row_news])
    weight_sq = jnp.stack([jnp.sum(member[0] * member[0]) for member in matrices + wide])
    stats = summed_over_all(
        col_parts + [row_totals, weight_sq, jnp.sum(norms * norms, 0), loss_part.reshape(1)], 2
    )
    updates = []
    cols_out = []
    for index, member in enumerate(matrices + wide):
        full_rows = member[0].shape[0] * devices
        cols_new = decay * member[3] + (1.0 - decay) * stats[index] / full_rows
        if index < 4:
            mean = stats[6][index] / full_rows
        else:
            mean = jnp.mean(cols_new)
        updates.append(member[1] * lax.rsqrt(row_news[index][:, None] * cols_new[None, :] / mean))
        cols_out.append(cols_new)
    moment_new = decay * norm_moment + (1.0 - decay) * (norm_g * norm_g + SQUARE_FLOOR)
    norm_update = norm_g * lax.rsqrt(moment_new)
    update_sq = jnp.stack([jnp.sum(update * update) for update in updates])
    totals = summed_over_all([update_sq, jnp.sum(norm_update * norm_update, 0)], 3)
    news = []
    for index, member in enumerate(matrices + wide):
        entries = member[0].shape[0] * member[0].shape[1] * devices
        clip = jnp.maximum(1.0, jnp.sqrt(totals[0][index] / entries))
        news.append(
            member[0] - learn_rate * jnp.sqrt(stats[7][index] / entries) * updates[index] / clip
        )
    norm_rows = norms.shape[0] * devices
    norm_clip = jnp.maximum(1.0, jnp.sqrt(totals[1] / norm_rows))
    norm_new = norms - learn_rate * jnp.sqrt(stats[8] / norm_rows) * norm_update / norm_clip
    return (
        stats[9][0],
        mask_count,
        table_g.T,
        place_g.T,
        qkv_g,
        out_g,
        in_g,
        down_g,
        norm_g,
        cols_out[4],
        row_news[4],
        cols_out[5],
        row_news[5],
        row_news[0],
        cols_out[0],
        row_news[1],
        cols_out[1],
        row_news[2],
        cols_out[2],
        row_news[3],
        cols_out[3],
        moment_new,
        news[4].T,
        news[5].T,
        news[0],
        news[1],
        news[2],
        news[3],
        norm_new,
    )


def solution(mesh):
    split, wide = P(("dp", "seq"), None), P(None, ("dp", "seq"))
    shard, same = P(("dp", "seq")), P()
    return jax.shard_map(
        functools.partial(on_device, (mesh.shape["dp"], mesh.shape["seq"])),
        mesh=mesh,
        in_specs=(P("dp", "seq"),) * 3
        + (P("dp"),)
        + (split,) * 3
        + (shard,)
        + (wide,) * 2
        + (split,) * 5
        + (same, shard) * 2
        + (shard, same) * 4
        + (split,),
        out_specs=(same, same)
        + (wide,) * 2
        + (split,) * 5
        + (same, shard) * 2
        + (shard, same) * 4
        + (split,)
        + (wide,) * 2
        + (split,) * 5,
        check_vma=False,
    )
```

time: 1550 us -> 567 us (0.37)
  waiting for transfers between devices: 886 us -> 0.01 us
  Pallas kernels: 0 us -> 265 us
  blocking collectives: 206 us -> 0 us
  local copies, waits for them, and re-layouts: 114 us -> 58.4 us
  matrix products: 176 us -> 124 us
  other arithmetic: 103 us -> 85 us
    reduce_scatter x4 -> x0, waiting for transfers between devices: 397 us -> none  [the longest x1 140 us: reduce_once(): lax.psum_scatter(grads[5], ('dp', 'seq'), scatter_dimension=0, tiled=True)]
    pallas_call x0 -> x4, Pallas kernels: none -> 265 us  [the longest x1 137 us: reduce_grads(): pl.pallas_call(reduce_kernel, out_shape=[jax.ShapeDtypeStruct(shape, F32)...]
    unnamed x13 -> x0, waiting for transfers between devices: 260 us -> none
    all_gather x5 -> x0, waiting for transfers between devices: 183 us -> none  [the longest x1 63.6 us: on_device(): lax.all_gather(in_weight.astype(jnp.bfloat16), ('dp', 'seq'), axis=0, til...]
    all_gather x2 -> x0, blocking collectives: 83.9 us -> none  [the longest x1 43.7 us: on_device(): lax.all_gather(norms.astype(jnp.bfloat16), ('dp', 'seq'), axis=0, tiled=T...]
    psum x2 -> x0, blocking collectives: 79.6 us -> none  [the longest x1 39.8 us: on_device(): lax.psum((col_parts[0], col_parts[1], col_parts[2], col_parts[3], wide_pa...]
    dot_general x42 -> x28, matrix products: 176 us -> 124 us  [the longest x16 92.8 us: mm(): lax.dot_general(left, right, ((sides[:1], sides[1:]), ((), ())), preferre...]
    all_to_all x4 -> x1, waiting for transfers between devices: 45.7 us -> 0.01 us  [on_device(): lax.all_to_all(jnp.concatenate((long_pack, short_pack[1:]), 0), 'seq', sp...]
  transfers between devices with their start and end apart: 15 -> 1, of which waited for: 11 -> 0; matrix products, arithmetic and copies ran while one was open for 16% -> 2% of each run, Pallas kernels for 0% -> 17%
where the time goes in v1:
time: 567 us; the launch traced here: 556 us
  Pallas kernels  265 us (47%)
  matrix products  124 us (22%)
  other arithmetic  85 us (15%)
  local copies, waits for them, and re-layouts  58.4 us (10%)
  between operations  18.9 us (3%)
    pallas_call x1, Pallas kernels, reduce_grads(): pl.pallas_call(reduce_kernel, out_shape=[jax.ShapeDtypeStruct(shape, F32)...  137 us
    pallas_call x1, Pallas kernels, gather_weights(): pl.pallas_call(gather_kernel, out_shape=[jax.ShapeDtypeStruct((32 * size,...  94.4 us
    dot_general x16, matrix products, mm(): lax.dot_general(left, right, ((sides[:1], sides[1:]), ((), ())), preferre...  92.8 us
    pallas_call x2, Pallas kernels, total_of(): pl.pallas_call(total_kernel, out_shape=jax.ShapeDtypeStruct(array.shape,...  33.6 us
    unnamed x281, local copies, waits for them, and re-layouts  21.2 us
    concatenate x2, local copies, waits for them, and re-layouts, summed_over_all(): flat = jnp.concatenate((flat, jnp.zeros((room,), F32))).reshape(-1, 128)  13.5 us
    dot_general x2, matrix products, attend_back(): jnp.einsum('qhe,khe->hqk', grad_mix, value, preferred_element_type=F32)  11.7 us
  transfers between devices with their start and end apart: 1, of which 0 were waited for; matrix products, arithmetic and copies ran while one was open for 2% of the time, Pallas kernels for 17%

profile of v1, /device:TPU:0, one launch (start us, length us, event | category | flops | bytes accessed | tf_op | source)
XLA Modules:
  0.0 555.7 jit_solution(13452309445072692652)
XLA Ops:
  1.5 1.4 fusion.113
  3.6 1.4 fusion.112
  7.7 4.2 all-to-all-start
  20.0 94.4 %shard_map.491 = (bf16[768,4864]{1,0:T(8,128)(2,1)}, bf16[768,2304]{1,0:T(8,128)(2,1)S(1)}, bf16[768,768]{1,0:T(8,128)(2,1)S(1)}, bf16[768,3072]{1,0:T(8,128)(2,1)}, bf16[3072,768]{1,0:T(8,128)(2,1)}) custom-call(f32[24,4864]{1,0:T(8,128)S(1)} %concatenate.33.refs_0_, f32[24,2304]{1,0:T(8,128)S(1)} %copy-done.4, f32[24,768]{1,0:T(8,128)S(1)} %copy-done.6, ...), custom_call_target="tpu_custom_call" | custom-call | tf_op jit(solution)/shard_map/pallas_call | solution.py:261
  114.4 1.8 copy-done.8
  117.2 1.1 convert_reduce_fusion
  123.2 1.6 slice_reduce_fusion.1
  128.0 1.2 add_reduce_fusion
  129.2 9.7 %fusion.118 = (f32[640]{0:T(1024)S(1)}, f32[640,768]{1,0:T(8,128)S(1)}) fusion(bf16[768,4864]{1,0:T(8,128)(2,1)} %get-tuple-element.39, s32[640]{0:T(1024)S(1)} %fusion.75, s32[640]{0:T(1024)S(1)} %bitcast.202), kind=kOutput, calls=%fused_computation.266 | convolution fusion | flops 4791336448 | bytes 9444864 | tf_op jit(solution)/shard_map/dot_general | solution.py:711
  139.4 3.1 convolution_convert_fusion.3
  142.5 1.5 slice.272
  144.9 2.8 copy.144
  149.5 2.1 fusion.25
  151.6 3.7 fusion.5
  157.0 5.3 fusion.38
  162.2 2.1 copy.146
  164.4 1.5 fusion.119
  166.8 1.3 convolution_convert_fusion.7
  168.3 1.2 fusion.120
  170.0 6.5 %multiply_convert_fusion.2 = (bf16[640,3072]{1,0:T(8,128)(2,1)S(1)}, f32[640,3072]{1,0:T(8,128)}) fusion(bf16[768,3072]{1,0:T(8,128)(2,1)S(1)} %bitcast.213, f32[640,768]{1,0:T(8,128)S(1)} %get-tuple-element.291, f32[768]{0:T(1024)S(1)} %copy-done.99, f32[768]{0:T(1024)S(1)} %copy-done.72, f32[640]{0:T(1024)S(1)} %add_rsqrt_fusion.1, ...), kind=kOutput, calls=%fused_computation.30 | convolution fusion | flops 3032186880 | bytes 18492416 | tf_op jit(solution)/shard_map/dot_general | solution.py:711
  176.6 3.4 fusion.121
  181.8 5.1 select_reduce_fusion.1
  187.0 4.7 select_reduce_fusion
  192.3 1.3 sub.203
  193.6 1.3 multiply_reduce_fusion.28
  194.9 8.0 %multiply_convert_fusion.1 = bf16[640,4864]{1,0:T(8,128)(2,1)S(1)} fusion(f32[640,4864]{1,0:T(8,128)} %copy-done.12, f32[640]{0:T(1024)S(1)} %bitcast.205, s32[640]{0:T(1024)} %bitcast.198, f32[640]{0:T(1024)} %get-tuple-element.249, pred[4864]{0:T(1024)(128)(4,1)S(1)} %iota_compare_fusion.3), kind=kLoop, calls=%fused_computation.11 | loop fusion | flops 21790720 | bytes 18690304 | tf_op jit(solution)/shard_map/convert_element_type | solution.py:841
  202.9 11.1 %multiply_reduce_fusion.1 = (bf16[768]{0:T(1024)(128)(2,1)}, f32[640]{0:T(1024)S(1)}, f32[640]{0:T(1024)S(1)}, bf16[768]{0:T(1024)(128)(2,1)}, f32[640,768]{1,0:T(8,128)S(1)}) fusion(f32[640,768]{1,0:T(8,128)S(1)} %copy-done.14, f32[640]{0:T(1024)S(1)} %copy-done.60, f32[640]{0:T(1024)S(1)} %broadcast_multiply_fusion.6, f32[768]{0:T(1024)S(1)} %get-tuple-element.212, ...), kind=kOutput, calls=%fused_computation.47 | convolution fusion | flops 4785927168 | bytes 17645568 | tf_op jit(solution)/shard_map/dot_general | solution.py:711
  214.6 1.5 copy-done.119
  216.1 5.6 %convolution_convert_fusion.refs_4_ = bf16[3072,768]{1,0:T(8,128)(2,1)} fusion(bf16[640,3072]{1,0:T(8,128)(2,1)S(1)} %copy-done.119, f32[640,768]{1,0:T(8,128)S(1)} %subtract_multiply_fusion.1), kind=kOutput, calls=%fused_computation.37 | convolution fusion | flops 3022749696 | bytes 10616832 | tf_op jit(solution)/shard_map/dot_general | solution.py:711
  221.8 6.3 %fusion.18 = bf16[640,3072]{1,0:T(8,128)(2,1)} fusion(f32[640,3072]{1,0:T(8,128)S(1)} %bitcast.225, bf16[3072,768]{1,0:T(8,128)(2,1)S(1)} %bitcast.219, f32[640,768]{1,0:T(8,128)S(1)} %subtract_multiply_fusion.1), kind=kOutput, calls=%fused_computation.29 | convolution fusion | flops 3040051200 | bytes 18481152 | tf_op jit(solution)/shard_map/dot_general | solution.py:711
  228.2 8.5 %convolution_convert_fusion.1.refs_3_ = bf16[768,3072]{1,0:T(8,128)(2,1)} fusion(bf16[640,3072]{1,0:T(8,128)(2,1)} %fusion.18, f32[640,768]{1,0:T(8,128)S(1)} %copy-done.21, f32[768]{0:T(1024)S(1)} %copy-done.100, f32[768]{0:T(1024)S(1)} %copy-done.73, f32[640]{0:T(1024)S(1)} %copy-done.78, f32[640]{0:T(1024)S(1)} %copy-done.58), kind=kOutput, calls=%fused_computation.38 | convolution fusion | flops 3024715776 | bytes 10628096 | tf_op jit(solution)/shard_map/dot_general | solution.py:711
  236.7 3.8 multiply_reduce_fusion.2
  241.8 2.1 convolution_convert_fusion.4.refs_2_
  246.8 1.4 copy.148
  248.3 11.3 %multiply_reduce_fusion = (f32[12,512]{1,0:T(8,128)S(1)}, f32[12,512,512]{1,2,0:T(8,128)}) fusion(f32[12,512]{1,0:T(8,128)S(1)} %copy-done.46, f32[12,512,512]{1,2,0:T(8,128)} %copy-done.11, pred[512,512]{0,1:T(8,128)(4,1)S(1)} %copy-done.23, bf16[512,12,64]{0,2,1:T(8,128)(2,1)S(1)} %bitcast.179, bf16[512,3,12,64]{0,3,2,1:T(8,128)(2,1)S(1)} %bitcast.175), kind=kOutput, calls=%fused_computation.1 | convolution fusion | flops 418375680 | bytes 27058176 | tf_op jit(solution)/shard_map/qhe,khe->hqk/dot_general | solution.py:734
  259.7 1.5 slice-done.2
  261.1 7.0 %multiply_convert_fusion = bf16[12,512,512]{1,2,0:T(8,128)(2,1)S(1)} fusion(f32[12,512,512]{1,2,0:T(8,128)} %get-tuple-element.303, f32[12,512]{1,0:T(8,128)S(1)} %get-tuple-element.302, f32[12,512]{1,0:T(8,128)S(1)} %copy-done.46, f32[12,512,512]{1,2,0:T(8,128)S(1)} %bitcast.172, pred[512,512]{0,1:T(8,128)(4,1)S(1)} %copy-done.23), kind=kLoop, calls=%fused_computation | loop fusion | flops 18874368 | bytes 31768576 | tf_op jit(solution)/shard_map/convert_element_type | solution.py:735
  268.1 2.0 fusion.42
  270.2 2.9 fusion.43
  273.1 3.4 fusion.39
  278.7 1.1 copy-done.19
  279.9 5.2 convolution_convert_fusion.2.refs_1_
  285.1 4.5 multiply_reduce_fusion.3
  289.6 7.2 %fusion.6 = bf16[640,4864]{1,0:T(8,128)(2,1)} fusion(s32[640]{0:T(1024)S(1)} %copy-done.76, s32[640]{0:T(1024)S(1)} %bitcast.203), kind=kLoop, calls=%fused_computation.20 | loop fusion | flops 12451840 | bytes 6231040 | tf_op jit(solution)/shard_map/convert_element_type | solution.py:818
  297.1 2.1 multiply_convert_fusion.3
  299.2 15.6 %fusion.10 = bf16[768,4864]{1,0:T(8,128)(2,1)} fusion(bf16[640,4864]{1,0:T(8,128)(2,1)} %fusion.6, bf16[640,4864]{1,0:T(8,128)(2,1)} %copy-done.24, bf16[640,768]{1,0:T(8,128)(2,1)S(1)} %multiply_convert_fusion.3, bf16[640,768]{1,0:T(8,128)(2,1)S(1)} %copy-done.41), kind=kOutput, calls=%fused_computation.23 | convolution fusion | flops 9595584512 | bytes 21889024 | tf_op jit(solution)/shard_map/dot_general | solution.py:711
  314.8 3.7 dynamic_update_slice.3.refs_0_
  318.7 137.3 %shard_map.492 = (f32[24,4864]{1,0:T(8,128)}, f32[24,2304]{1,0:T(8,128)}, f32[24,768]{1,0:T(8,128)}, f32[24,3072]{1,0:T(8,128)}, f32[96,768]{1,0:T(8,128)}) custom-call(bf16[768,4864]{1,0:T(8,128)(2,1)} %dynamic_update_slice.3.refs_0_, bf16[768,2304]{1,0:T(8,128)(2,1)} %convolution_convert_fusion.2.refs_1_, ...), custom_call_target="tpu_custom_call" | custom-call | tf_op jit(solution)/shard_map/pallas_call | solution.py:621
  456.1 1.3 fusion.60
  458.4 1.1 fusion.62
  461.6 1.1 fusion.64
  465.2 9.0 %concatenate.38 = f32[12288]{0:T(1024)} concatenate(f32[2304]{0:T(1024)S(1)} %get-tuple-element.223, f32[768]{0:T(1024)S(1)} %get-tuple-element.225, f32[3072]{0:T(1024)S(1)} %get-tuple-element.221, f32[768]{0:T(1024)S(1)} %get-tuple-element.219, f32[4101]{0:T(1024)S(1)} %get-tuple-element.211, f32[512]{0:T(512)S(1)} %get-tuple-element.209, f32[1]{0:T(128)} %bitcast.37, ...), dimensions={0} | concatenate | bytes 98304 | tf_op jit(solution)/shard_map/concatenate | solution.py:885
  474.2 18.9 %shard_map.493 = f32[96,128]{1,0:T(8,128)} custom-call(f32[96,128]{1,0:T(8,128)} %bitcast.197), custom_call_target="tpu_custom_call" | custom-call | tf_op jit(solution)/shard_map/pallas_call | solution.py:670
  493.1 1.7 fusion.114
  494.8 1.4 fusion.101
  496.2 1.4 fusion.103
  504.5 1.5 multiply_reduce_fusion.24
  506.0 1.8 multiply_reduce_fusion.14
  507.8 1.8 multiply_reduce_fusion.16
  509.6 1.7 multiply_reduce_fusion.17
  511.3 1.6 multiply_reduce_fusion.22
  513.6 4.5 concatenate.39
  518.1 14.7 %shard_map.494 = f32[8,128]{1,0:T(8,128)} custom-call(f32[8,128]{1,0:T(8,128)} %bitcast.204), custom_call_target="tpu_custom_call" | custom-call | tf_op jit(solution)/shard_map/pallas_call | solution.py:670
  532.8 1.6 fusion.115
  (380 shorter events, 54.8 us)
Async XLA Ops:
  0.7 121.8 %copy-start.81 = (f32[24,6]{0,1:T(8,128)S(1)}, f32[24,6]{0,1:T(8,128)}, u32[]{:S(2)}) copy-start(f32[24,6]{0,1:T(8,128)} %param.42) | copy-start | bytes 1732
  0.7 120.5 %copy-start.28 = (f32[4101,24]{0,1:T(8,128)S(1)}, f32[4101,24]{0,1:T(8,128)}, u32[]{:S(2)}) copy-start(f32[4101,24]{0,1:T(8,128)} %param.36) | copy-start | bytes 1181092
  0.7 121.2 %copy-start.42 = (f32[512,24]{0,1:T(8,128)S(1)}, f32[512,24]{0,1:T(8,128)}, u32[]{:S(2)}) copy-start(f32[512,24]{0,1:T(8,128)} %param.37) | copy-start | bytes 147460
  7.7 120.3 %all-to-all-start = ((s32[4,4,128]{2,1,0:T(4,128)}), s32[4,4,128]{2,1,0:T(4,128)S(1)}, u32[]{:S(2)}, u32[]{:S(2)}) async-start(s32[4,4,128]{2,1,0:T(4,128)} %pad_add_fusion), calls=%async_computation | async-start | bytes 16384 | tf_op jit(solution)/shard_map/all_to_all | solution.py:784
  20.0 106.0 %copy-start.101 = (f32[24,6]{0,1:T(8,128)S(1)}, f32[24,6]{0,1:T(8,128)}, u32[]{:S(2)}) copy-start(f32[24,6]{0,1:T(8,128)} %param.55) | copy-start | bytes 1732
  123.2 15.7 %copy-start.75 = (s32[640]{0:T(1024)}, s32[640]{0:T(1024)S(1)}, u32[]{:S(2)}) copy-start(s32[640]{0:T(1024)S(1)} %fusion.75) | copy-start | bytes 7684
  124.8 14.6 %copy-start.82 = (f32[768]{0:T(1024)}, f32[768]{0:T(1024)S(1)}, u32[]{:S(2)}) copy-start(f32[768]{0:T(1024)S(1)} %get-tuple-element.217) | copy-start | bytes 9220
  124.8 14.6 %copy-start.96 = (f32[768]{0:T(1024)}, f32[768]{0:T(1024)S(1)}, u32[]{:S(2)}) copy-start(f32[768]{0:T(1024)S(1)} %get-tuple-element.216) | copy-start | bytes 9220
  128.0 10.9 %copy-start.56 = (s32[4,4,128]{2,1,0:T(4,128)}, s32[4,4,128]{2,1,0:T(4,128)S(1)}, u32[]{:S(2)}) copy-start(s32[4,4,128]{2,1,0:T(4,128)S(1)} %all-to-all-done) | copy-start | bytes 24580
  129.2 9.7 %copy-start.79 = (s32[5,128]{1,0:T(8,128)}, s32[5,128]{1,0:T(8,128)S(1)}, u32[]{:S(2)}) copy-start(s32[5,128]{1,0:T(8,128)S(1)} %get-tuple-element.227) | copy-start | bytes 7684
  129.2 10.2 %copy-start.9 = (bf16[768,2304]{1,0:T(8,128)(2,1)S(1)}, bf16[768,2304]{1,0:T(8,128)(2,1)}, u32[]{:S(2)}) copy-start(bf16[768,2304]{1,0:T(8,128)(2,1)} %copy-done.8) | copy-start | bytes 10616836
  139.0 29.3 %copy-start.63 = (f32[640]{0:T(1024)}, f32[640]{0:T(1024)S(1)}, u32[]{:S(2)}) copy-start(f32[640]{0:T(1024)S(1)} %broadcast_multiply_fusion.8) | copy-start | bytes 7684
  194.9 8.0 %copy-start.14 = (f32[640,768]{1,0:T(8,128)S(1)}, f32[640,768]{1,0:T(8,128)}, u32[]{:S(2)}) copy-start(f32[640,768]{1,0:T(8,128)} %copy-done.13) | copy-start | bytes 5898244
  194.9 8.0 %copy-start.60 = (f32[640]{0:T(1024)S(1)}, f32[640]{0:T(1024)}, u32[]{:S(2)}) copy-start(f32[640]{0:T(1024)} %copy-done.59) | copy-start | bytes 7684
  202.9 11.1 %copy-start.24 = (bf16[640,4864]{1,0:T(8,128)(2,1)}, bf16[640,4864]{1,0:T(8,128)(2,1)S(1)}, u32[]{:S(2)}) copy-start(bf16[640,4864]{1,0:T(8,128)(2,1)S(1)} %multiply_convert_fusion.1) | copy-start | bytes 18677764
  214.0 7.8 %slice-start.12 = ((s8[4718592]{0:T(1024)(128)(4,1)}), s8[4194304]{0:T(1024)(128)(4,1)S(1)}, s32[]{:S(2)}) async-start(s8[4718592]{0:T(1024)(128)(4,1)} %bitcast.218), calls=%async_computation.13 | async-start | bytes 8388608
  214.0 7.7 %slice-start.14 = ((s8[7864320]{0:T(1024)(128)(4,1)}), s8[3670016]{0:T(1024)(128)(4,1)S(1)}, s32[]{:S(2)}) async-start(s8[7864320]{0:T(1024)(128)(4,1)} %bitcast.224), calls=%async_computation.15 | async-start | bytes 7340032
  216.1 20.6 %slice-start.8 = ((s8[4718592]{0:T(1024)(128)(4,1)}), s8[4194304]{0:T(1024)(128)(4,1)S(1)}, s32[]{:S(2)}) async-start(s8[4718592]{0:T(1024)(128)(4,1)} %bitcast.214), calls=%async_computation.9 | async-start | bytes 8388608
  221.8 14.9 %slice-start.9 = ((s8[4718592]{0:T(1024)(128)(4,1)}), s8[524288]{0:T(1024)(128)(4,1)S(1)}, s32[]{:S(2)}) async-start(s8[4718592]{0:T(1024)(128)(4,1)} %bitcast.214), calls=%async_computation.10 | async-start | bytes 1048576
  228.2 8.5 %copy-start.120 = (bf16[640,3072]{1,0:T(8,128)(2,1)S(1)}, bf16[640,3072]{1,0:T(8,128)(2,1)}, u32[]{:S(2)}) copy-start(bf16[640,3072]{1,0:T(8,128)(2,1)} %fusion.18) | copy-start | bytes 11796484
  248.2 11.4 %copy-start.31 = (bf16[512,768]{0,1:T(8,128)(2,1)}, bf16[512,768]{0,1:T(8,128)(2,1)S(1)}, u32[]{:S(2)}) copy-start(bf16[512,768]{0,1:T(8,128)(2,1)S(1)} %copy.148) | copy-start | bytes 2359300
  248.3 11.4 %slice-start = ((s8[12582912]{0:T(1024)(128)(4,1)}), s8[4194304]{0:T(1024)(128)(4,1)S(1)}, s32[]{:S(2)}) async-start(s8[12582912]{0:T(1024)(128)(4,1)} %bitcast.171), calls=%async_computation.1 | async-start | bytes 8388608
  248.3 11.4 %slice-start.1 = ((s8[12582912]{0:T(1024)(128)(4,1)}), s8[4194304]{0:T(1024)(128)(4,1)S(1)}, s32[]{:S(2)}) async-start(s8[12582912]{0:T(1024)(128)(4,1)} %bitcast.171), calls=%async_computation.2 | async-start | bytes 8388608
  248.3 12.9 %slice-start.2 = ((s8[12582912]{0:T(1024)(128)(4,1)}), s8[4194304]{0:T(1024)(128)(4,1)S(1)}, s32[]{:S(2)}) async-start(s8[12582912]{0:T(1024)(128)(4,1)} %bitcast.171), calls=%async_computation.3 | async-start | bytes 8388608
  289.6 7.2 %copy-start.107 = (bf16[768]{0:T(1024)(128)(2,1)S(1)}, bf16[768]{0:T(1024)(128)(2,1)}, u32[]{:S(2)}) copy-start(bf16[768]{0:T(1024)(128)(2,1)} %get-tuple-element.196) | copy-start | bytes 4612
  289.6 7.2 %copy-start.106 = (bf16[768]{0:T(1024)(128)(2,1)S(1)}, bf16[768]{0:T(1024)(128)(2,1)}, u32[]{:S(2)}) copy-start(bf16[768]{0:T(1024)(128)(2,1)} %get-tuple-element.205) | copy-start | bytes 4612
  318.5 144.2 %copy-start.108 = (f32[24]{0:T(128)S(1)}, f32[24]{0:T(128)}, u32[]{:S(2)}) copy-start(f32[24]{0:T(128)} %param.47) | copy-start | bytes 292
  318.5 144.8 %copy-start.109 = (f32[96]{0:T(128)S(1)}, f32[96]{0:T(128)}, u32[]{:S(2)}) copy-start(f32[96]{0:T(128)} %param.53) | copy-start | bytes 1156
  318.5 145.4 %copy-start.110 = (f32[24]{0:T(128)S(1)}, f32[24]{0:T(128)}, u32[]{:S(2)}) copy-start(f32[24]{0:T(128)} %param.46) | copy-start | bytes 292
  318.5 145.4 %copy-start.111 = (f32[24]{0:T(128)S(1)}, f32[24]{0:T(128)}, u32[]{:S(2)}) copy-start(f32[24]{0:T(128)} %param.44) | copy-start | bytes 292
  318.6 146.0 %copy-start.112 = (f32[24]{0:T(128)S(1)}, f32[24]{0:T(128)}, u32[]{:S(2)}) copy-start(f32[24]{0:T(128)} %param.51) | copy-start | bytes 292
  318.6 146.0 %copy-start.113 = (f32[24]{0:T(128)S(1)}, f32[24]{0:T(128)}, u32[]{:S(2)}) copy-start(f32[24]{0:T(128)} %param.49) | copy-start | bytes 292
  318.6 146.6 %copy-start.104 = (f32[6]{0:T(128)S(1)}, f32[6]{0:T(128)}, u32[]{:S(2)}) copy-start(f32[6]{0:T(128)} %multiply_reduce_fusion.27) | copy-start | bytes 76
  318.6 176.2 %copy-start.105 = (f32[512]{0:T(512)S(1)}, f32[512]{0:T(512)}, u32[]{:S(2)}) copy-start(f32[512]{0:T(512)} %param.45) | copy-start | bytes 6148
  318.6 177.6 %copy-start.70 = (f32[4101]{0:T(1024)S(1)}, f32[4101]{0:T(1024)}, u32[]{:S(2)}) copy-start(f32[4101]{0:T(1024)} %param.43) | copy-start | bytes 49216
  318.6 178.9 %copy-start.88 = (f32[3072]{0:T(1024)S(1)}, f32[3072]{0:T(1024)}, u32[]{:S(2)}) copy-start(f32[3072]{0:T(1024)} %param.52) | copy-start | bytes 36868
  318.6 180.9 %copy-start.89 = (f32[2304]{0:T(1024)S(1)}, f32[2304]{0:T(1024)}, u32[]{:S(2)}) copy-start(f32[2304]{0:T(1024)} %param.48) | copy-start | bytes 27652
  318.6 182.3 %copy-start.55 = (f32[24,6]{1,0:T(8,128)S(1)}, f32[24,6]{1,0:T(8,128)}, u32[]{:S(2)}) copy-start(f32[24,6]{1,0:T(8,128)} %copy.157) | copy-start | bytes 1732
  318.7 184.4 %copy-start.102 = (f32[768]{0:T(1024)S(1)}, f32[768]{0:T(1024)}, u32[]{:S(2)}) copy-start(f32[768]{0:T(1024)} %param.54) | copy-start | bytes 9220
  318.7 184.4 %copy-start.103 = (f32[768]{0:T(1024)S(1)}, f32[768]{0:T(1024)}, u32[]{:S(2)}) copy-start(f32[768]{0:T(1024)} %param.50) | copy-start | bytes 9220
  455.9 56.9 %copy-start.30 = (f32[24,2304]{1,0:T(8,128)S(1)}, f32[24,2304]{1,0:T(8,128)}, u32[]{:S(2)}) copy-start(f32[24,2304]{1,0:T(8,128)} %get-tuple-element.342) | copy-start | bytes 663556
  456.0 86.2 %copy-start.27 = (f32[24,4864]{1,0:T(8,128)S(1)}, f32[24,4864]{1,0:T(8,128)}, u32[]{:S(2)}) copy-start(f32[24,4864]{1,0:T(8,128)} %get-tuple-element.48) | copy-start | bytes 1400836
  456.0 86.1 %copy-start.53 = (f32[24,6]{1,0:T(8,128)S(1)}, f32[24,6]{1,0:T(8,128)}, u32[]{:S(2)}) copy-start(f32[24,6]{1,0:T(8,128)} %copy-done.52) | copy-start | bytes 1732
  456.0 90.3 %copy-start.1 = (f32[96,768]{1,0:T(8,128)S(1)}, f32[96,768]{1,0:T(8,128)}, u32[]{:S(2)}) copy-start(f32[96,768]{1,0:T(8,128)} %refs_4_.1) | copy-start | bytes 884740
  456.0 90.3 %copy-start.25 = (f32[96,768]{1,0:T(8,128)S(1)}, f32[96,768]{1,0:T(8,128)}, u32[]{:S(2)}) copy-start(f32[96,768]{1,0:T(8,128)} %get-tuple-element.345) | copy-start | bytes 884740
  456.0 91.2 %copy-start.3 = (f32[24,3072]{1,0:T(8,128)S(1)}, f32[24,3072]{1,0:T(8,128)}, u32[]{:S(2)}) copy-start(f32[24,3072]{1,0:T(8,128)} %refs_3_.1) | copy-start | bytes 884740
  456.0 91.2 %copy-start.26 = (f32[24,3072]{1,0:T(8,128)S(1)}, f32[24,3072]{1,0:T(8,128)}, u32[]{:S(2)}) copy-start(f32[24,3072]{1,0:T(8,128)} %get-tuple-element.344) | copy-start | bytes 884740
  456.0 92.0 %copy-start.7 = (f32[24,768]{1,0:T(8,128)S(1)}, f32[24,768]{1,0:T(8,128)}, u32[]{:S(2)}) copy-start(f32[24,768]{1,0:T(8,128)} %refs_2_.1) | copy-start | bytes 221188
  456.0 92.0 %copy-start.38 = (f32[24,768]{1,0:T(8,128)S(1)}, f32[24,768]{1,0:T(8,128)}, u32[]{:S(2)}) copy-start(f32[24,768]{1,0:T(8,128)} %get-tuple-element.343) | copy-start | bytes 221188
  456.0 92.7 %copy-start.5 = (f32[24,2304]{1,0:T(8,128)S(1)}, f32[24,2304]{1,0:T(8,128)}, u32[]{:S(2)}) copy-start(f32[24,2304]{1,0:T(8,128)} %refs_1_.1) | copy-start | bytes 663556
  456.1 93.5 %copy-start.43 = (f32[512,24]{0,1:T(8,128)S(1)}, f32[512,24]{0,1:T(8,128)}, u32[]{:S(2)}) copy-start(f32[512,24]{0,1:T(8,128)} %param.37) | copy-start | bytes 147460
  457.4 92.9 %copy-start.29 = (f32[4101,24]{0,1:T(8,128)S(1)}, f32[4101,24]{0,1:T(8,128)}, u32[]{:S(2)}) copy-start(f32[4101,24]{0,1:T(8,128)} %param.36) | copy-start | bytes 1181092
  463.4 87.9 %copy-start.95 = (f32[24]{0:T(128)}, f32[24]{0:T(128)S(1)}, u32[]{:S(2)}) copy-start(f32[24]{0:T(128)S(1)} %get-tuple-element.351) | copy-start | bytes 292
  464.0 87.3 %copy-start.90 = (f32[96]{0:T(128)}, f32[96]{0:T(128)S(1)}, u32[]{:S(2)}) copy-start(f32[96]{0:T(128)S(1)} %get-tuple-element.357) | copy-start | bytes 1156
  464.6 86.7 %copy-start.91 = (f32[24]{0:T(128)}, f32[24]{0:T(128)S(1)}, u32[]{:S(2)}) copy-start(f32[24]{0:T(128)S(1)} %get-tuple-element.348) | copy-start | bytes 292
  464.6 86.7 %copy-start.93 = (f32[24]{0:T(128)}, f32[24]{0:T(128)S(1)}, u32[]{:S(2)}) copy-start(f32[24]{0:T(128)S(1)} %get-tuple-element.350) | copy-start | bytes 292
  465.2 86.1 %copy-start.92 = (f32[24]{0:T(128)}, f32[24]{0:T(128)S(1)}, u32[]{:S(2)}) copy-start(f32[24]{0:T(128)S(1)} %get-tuple-element.355) | copy-start | bytes 292
  465.2 86.1 %copy-start.94 = (f32[24]{0:T(128)}, f32[24]{0:T(128)S(1)}, u32[]{:S(2)}) copy-start(f32[24]{0:T(128)S(1)} %get-tuple-element.353) | copy-start | bytes 292
  496.2 55.1 %copy-start.71 = (f32[512]{0:T(512)}, f32[512]{0:T(512)S(1)}, u32[]{:S(2)}) copy-start(f32[512]{0:T(512)S(1)} %get-tuple-element.349) | copy-start | bytes 6148
  497.5 53.8 %copy-start.48 = (f32[4101]{0:T(1024)}, f32[4101]{0:T(1024)S(1)}, u32[]{:S(2)}) copy-start(f32[4101]{0:T(1024)S(1)} %get-tuple-element.347) | copy-start | bytes 49216
  498.3 53.1 %copy-start.51 = (f32[3072]{0:T(1024)}, f32[3072]{0:T(1024)S(1)}, u32[]{:S(2)}) copy-start(f32[3072]{0:T(1024)S(1)} %bitcast_add_fusion) | copy-start | bytes 36868
  500.3 51.0 %copy-start.54 = (f32[2304]{0:T(1024)}, f32[2304]{0:T(1024)S(1)}, u32[]{:S(2)}) copy-start(f32[2304]{0:T(1024)S(1)} %bitcast_add_fusion.1) | copy-start | bytes 27652
  503.8 47.6 %copy-start.61 = (f32[768]{0:T(1024)}, f32[768]{0:T(1024)S(1)}, u32[]{:S(2)}) copy-start(f32[768]{0:T(1024)S(1)} %get-tuple-element.358) | copy-start | bytes 9220
  503.8 47.6 %copy-start.62 = (f32[768]{0:T(1024)}, f32[768]{0:T(1024)S(1)}, u32[]{:S(2)}) copy-start(f32[768]{0:T(1024)S(1)} %get-tuple-element.354) | copy-start | bytes 9220
  (74 other events, 249.0 us)
